TPU v7x, 512 devices: a whole 4x4x16 slice. The times are simulated.
512 devices in a mesh: section: 64 (over y, z_lo, x), tp: 8 (over z_hi, core).
Axes of the slice: x: 4, y: 4, z: 16 (z_hi: 4, z_lo: 4; z = z_hi * 4 + z_lo), core: 2. Of those that a mesh axis runs over, the one named last changes fastest.
Arguments:
- fwd_q: bfloat16 [64, 128, 8192], P('section', None, 'tp'), may hold values from -4.5 to 4.5
- fwd_k: bfloat16 [64, 128, 1024], P('section', None, 'tp'), may hold values from -4.5 to 4.5
- fwd_v: bfloat16 [64, 128, 1024], P('section', None, 'tp'), may hold values from -6 to 6
- fwd_segments: int32 [64, 128], P('section'), may hold values from 0 to 3, never falling along the last dimension, each value on 1 to 64 neighbouring positions
- held_q: bfloat16 [64, 128, 8192], P('section', None, 'tp'), may hold values from -4.5 to 4.5
- held_k: bfloat16 [64, 128, 1024], P('section', None, 'tp'), may hold values from -4.5 to 4.5
- held_v: bfloat16 [64, 128, 1024], P('section', None, 'tp'), may hold values from -6 to 6
- back_segments: int32 [64, 128], P('section'), may hold values from 0 to 3, never falling along the last dimension, each value on 1 to 64 neighbouring positions
- up_grad: bfloat16 [64, 128, 8192], P('section', None, 'tp'), may hold values from -6 to 6
Outputs:
- passed_output: bfloat16 [64, 128, 8192], P('section', 'tp')
- evicted_q: bfloat16 [64, 128, 8192], P('section', None, 'tp')
- evicted_k: bfloat16 [64, 128, 1024], P('section', None, 'tp')
- evicted_v: bfloat16 [64, 128, 1024], P('section', None, 'tp')
- grad_q: bfloat16 [64, 128, 8192], P('section', None, 'tp')
- grad_k: bfloat16 [64, 128, 1024], P('section', None, 'tp')
- grad_v: bfloat16 [64, 128, 1024], P('section', None, 'tp')
Inputs may be any that keep to these rules, and one draw needn't show every extreme that they name: `fwd_segments`: document numbers never fall along a micro-batch; each document has 1 to 64 tokens. `back_segments`: document numbers never fall along a micro-batch; each document has 1 to 64 tokens.
All inputs are finite; a program needn't handle non-finite values.
Results may differ from a plain program's by a relative error of at most 0.0058.
Values may be sent and summed in bfloat16 or wider, within the bound.
No kernel may reach another device: no remote copies, remote signals or barrier semaphores. Data moves between devices by JAX's collectives and lax.ppermute only.
A program may use at most 64 MiB of HBM per device.

v0:
```python
import jax
import jax.numpy as jnp
from jax import lax
from jax.sharding import PartitionSpec as P

HQ = 64
KV = 8
HD = 128


def shifted_2(value, axis, steps):
    count = lax.axis_size(axis)
    pairs = [(source, (source + steps) % count) for source in range(count)]
    return lax.ppermute(value, axis, pairs)


def split_heads(queries, key_rows, value_rows):
    row_count = queries.shape[0]
    kv_local = key_rows.shape[1] // HD
    group_size = HQ // KV
    query_heads = queries.reshape(row_count, kv_local, group_size, HD)
    key_heads = key_rows.reshape(row_count, kv_local, HD)
    value_heads = value_rows.reshape(row_count, kv_local, HD)
    return (query_heads, key_heads, value_heads)


def probability(query_heads, key_heads, segment_ids):
    row_count = query_heads.shape[0]
    scores = jnp.einsum(
        "qkgd,skd->kgqs", query_heads, key_heads, preferred_element_type=jnp.float32
    ) * HD ** (-0.5)
    positions = jnp.arange(row_count)
    allowed = (segment_ids[:, None] == segment_ids[None, :]) & (
        positions[:, None] >= positions[None, :]
    )
    scores = jnp.where(allowed, scores, -jnp.inf)
    row_max = jnp.max(scores, axis=-1, keepdims=True)
    weights = jnp.exp(scores - row_max)
    return weights / jnp.sum(weights, axis=-1, keepdims=True)


def forward(queries, key_rows, value_rows, segment_ids):
    query_heads, key_heads, value_heads = split_heads(queries, key_rows, value_rows)
    prob = probability(query_heads, key_heads, segment_ids)
    prob_low = prob.astype(jnp.bfloat16)
    result = jnp.einsum("kgqs,skd->qkgd", prob_low, value_heads, preferred_element_type=jnp.float32)
    return result.reshape(queries.shape[0], queries.shape[1]).astype(jnp.bfloat16)


def backward(queries, key_rows, value_rows, segment_ids, out_grad):
    row_count = queries.shape[0]
    query_heads, key_heads, value_heads = split_heads(queries, key_rows, value_rows)
    prob = probability(query_heads, key_heads, segment_ids)
    prob_low = prob.astype(jnp.bfloat16)
    grad_heads = out_grad.reshape(query_heads.shape)
    value_grad = jnp.einsum(
        "kgqs,qkgd->skd", prob_low, grad_heads, preferred_element_type=jnp.float32
    )
    dprob = jnp.einsum(
        "qkgd,skd->kgqs", grad_heads, value_heads, preferred_element_type=jnp.float32
    )
    delta = jnp.sum(prob * dprob, axis=-1, keepdims=True)
    dscore = (prob * (dprob - delta) * HD ** (-0.5)).astype(jnp.bfloat16)
    query_grad = jnp.einsum("kgqs,skd->qkgd", dscore, key_heads, preferred_element_type=jnp.float32)
    key_grad = jnp.einsum("kgqs,qkgd->skd", dscore, query_heads, preferred_element_type=jnp.float32)
    return (
        query_grad.reshape(row_count, queries.shape[1]).astype(jnp.bfloat16),
        key_grad.reshape(row_count, key_rows.shape[1]).astype(jnp.bfloat16),
        value_grad.reshape(row_count, key_rows.shape[1]).astype(jnp.bfloat16),
    )


def mirror_move(stash):
    section_count = lax.axis_size("section")
    row_count = stash.shape[0]
    width = stash.shape[1]
    pieces = stash.reshape(row_count, section_count, width // section_count)
    spread = lax.all_to_all(pieces, "section", split_axis=1, concat_axis=1, tiled=True)
    flipped = jnp.flip(spread, axis=1)
    collected = lax.all_to_all(flipped, "section", split_axis=1, concat_axis=1, tiled=True)
    return collected.reshape(row_count, width)


def shards(fwd_q, fwd_k, fwd_v, fwd_segments, held_q, held_k, held_v, back_segments, up_grad):
    query_width = fwd_q.shape[2]
    key_width = fwd_k.shape[2]
    held_stash = jnp.concatenate([held_q[0], held_k[0], held_v[0]], axis=1)
    held_stash = mirror_move(held_stash)
    out_local = forward(fwd_q[0], fwd_k[0], fwd_v[0], fwd_segments[0])
    fresh_stash = jnp.concatenate([fwd_q[0], fwd_k[0], fwd_v[0]], axis=1)
    fresh_stash = mirror_move(fresh_stash)
    arriving = shifted_2(up_grad[0], "section", -1)
    own_q = held_stash[:, :query_width]
    own_k = held_stash[:, query_width : query_width + key_width]
    own_v = held_stash[:, query_width + key_width :]
    grad_q, grad_k, grad_v = backward(own_q, own_k, own_v, back_segments[0], arriving)
    shifted = shifted_2(out_local, "section", 1)
    passed_output = lax.all_to_all(shifted, "tp", split_axis=0, concat_axis=1, tiled=True)
    evicted_q = fresh_stash[:, :query_width]
    evicted_k = fresh_stash[:, query_width : query_width + key_width]
    evicted_v = fresh_stash[:, query_width + key_width :]
    return (
        passed_output[None],
        evicted_q[None],
        evicted_k[None],
        evicted_v[None],
        grad_q[None],
        grad_k[None],
        grad_v[None],
    )


def solution(mesh):
    in_specs = (
        P("section", None, "tp"),
        P("section", None, "tp"),
        P("section", None, "tp"),
        P("section", None),
        P("section", None, "tp"),
        P("section", None, "tp"),
        P("section", None, "tp"),
        P("section", None),
        P("section", None, "tp"),
    )
    out_specs = (
        P("section", "tp", None),
        P("section", None, "tp"),
        P("section", None, "tp"),
        P("section", None, "tp"),
        P("section", None, "tp"),
        P("section", None, "tp"),
        P("section", None, "tp"),
    )
    return jax.shard_map(shards, mesh=mesh, in_specs=in_specs, out_specs=out_specs, check_vma=False)
```

profile of v0, /device:TPU:2, one launch (start us, length us, event | category | flops | bytes accessed | tf_op | source)
XLA Modules:
  0.0 139.7 jit_solution(15120969164779303540)
XLA Ops:
  0.6 1.0 copy.79
  3.8 3.4 %collective-permute-start = (bf16[128,1024]{1,0:T(8,128)(2,1)S(1)}, bf16[128,1024]{1,0:T(8,128)(2,1)}, u32[]{:S(2)}, u32[]{:S(2)}) collective-permute-start(bf16[128,1024]{1,0:T(8,128)(2,1)S(1)} %copy.49), channel_id=1, source_target_pairs={{0,8},{8,16},{16,24},{24,32},{32,40},{40,48},{48,56},{56,64},{64,7... | collective-permute-start | bytes 786440 | tf_op jit(solution)/shard_map/ppermute | solution.py:14
  7.2 8.9 %collective-permute-done = bf16[128,1024]{1,0:T(8,128)(2,1)} collective-permute-done((bf16[128,1024]{1,0:T(8,128)(2,1)S(1)}, bf16[128,1024]{1,0:T(8,128)(2,1)}, u32[]{:S(2)}, u32[]{:S(2)}) %collective-permute-start) | collective-permute-done | bytes 262176 | tf_op jit(solution)/shard_map/ppermute | solution.py:14
  16.1 13.0 %all-to-all-start = ((bf16[8,16,1024]{2,1,0:T(8,128)(2,1)}), bf16[8,16,1024]{2,1,0:T(8,128)(2,1)S(1)}, u32[]{:S(2)}, u32[]{:S(2)}) async-start(bf16[8,16,1024]{2,1,0:T(8,128)(2,1)} %bitcast.12), calls=%async_computation | async-start | bytes 524288 | tf_op jit(solution)/shard_map/all_to_all | solution.py:98
  29.4 0.8 reshape.160
  30.2 18.1 %all-to-all-done = bf16[8,16,1024]{2,1,0:T(8,128)(2,1)S(1)} async-done(((bf16[8,16,1024]{2,1,0:T(8,128)(2,1)}), bf16[8,16,1024]{2,1,0:T(8,128)(2,1)S(1)}, u32[]{:S(2)}, u32[]{:S(2)}) %all-to-all-start) | async-done | bytes 262176 | tf_op jit(solution)/shard_map/all_to_all | solution.py:98
  48.3 12.6 %all-to-all-start.3 = ((bf16[128,64,20]{0,2,1:T(8,128)(2,1)}), bf16[128,64,20]{0,2,1:T(8,128)(2,1)S(1)}, u32[]{:S(2)}, u32[]{:S(2)}) async-start(bf16[128,64,20]{0,2,1:T(8,128)(2,1)} %reshape.160), calls=%async_computation.3 | async-start | bytes 786432 | tf_op jit(solution)/shard_map/all_to_all | solution.py:78
  61.2 0.8 reshape.158
  62.0 11.8 %all-to-all-done.3 = bf16[128,64,20]{0,2,1:T(8,128)(2,1)S(1)} async-done(((bf16[128,64,20]{0,2,1:T(8,128)(2,1)}), bf16[128,64,20]{0,2,1:T(8,128)(2,1)S(1)}, u32[]{:S(2)}, u32[]{:S(2)}) %all-to-all-start.3) | async-done | bytes 327712 | tf_op jit(solution)/shard_map/all_to_all | solution.py:78
  73.8 6.0 %all-to-all-start.1 = ((bf16[128,64,20]{0,2,1:T(8,128)(2,1)}), bf16[128,64,20]{0,2,1:T(8,128)(2,1)S(1)}, u32[]{:S(2)}, u32[]{:S(2)}) async-start(bf16[128,64,20]{0,2,1:T(8,128)(2,1)} %reshape.158), calls=%async_computation.1 | async-start | bytes 786432 | tf_op jit(solution)/shard_map/all_to_all | solution.py:78
  79.9 0.8 rev.8
  80.6 12.7 %all-to-all-done.1 = bf16[128,64,20]{0,2,1:T(8,128)(2,1)S(1)} async-done(((bf16[128,64,20]{0,2,1:T(8,128)(2,1)}), bf16[128,64,20]{0,2,1:T(8,128)(2,1)S(1)}, u32[]{:S(2)}, u32[]{:S(2)}) %all-to-all-start.1) | async-done | bytes 327712 | tf_op jit(solution)/shard_map/all_to_all | solution.py:78
  93.3 6.0 %all-to-all-start.4 = ((bf16[128,64,20]{0,2,1:T(8,128)(2,1)}), bf16[128,64,20]{0,2,1:T(8,128)(2,1)S(1)}, u32[]{:S(2)}, u32[]{:S(2)}) async-start(bf16[128,64,20]{0,2,1:T(8,128)(2,1)} %rev.8), calls=%async_computation.4 | async-start | bytes 786432 | tf_op jit(solution)/shard_map/all_to_all | solution.py:80
  99.5 2.4 %collective-permute-start.1 = (bf16[128,1024]{0,1:T(8,128)(2,1)S(1)}, bf16[128,1024]{0,1:T(8,128)(2,1)S(1)}, u32[]{:S(2)}, u32[]{:S(2)}) collective-permute-start(bf16[128,1024]{0,1:T(8,128)(2,1)S(1)} %bitcast.130), channel_id=1, source_target_pairs={{0,504},{8,0},{16,8},{24,16},{32,24},{40,32},{48,40},{56,48},{64,5... | collective-permute-start | bytes 786440 | tf_op jit(solution)/shard_map/ppermute | solution.py:14
  102.2 0.8 broadcast_in_dim.38
  103.0 0.8 rev.7
  103.8 9.2 %all-to-all-done.4 = bf16[128,64,20]{0,2,1:T(8,128)(2,1)S(1)} async-done(((bf16[128,64,20]{0,2,1:T(8,128)(2,1)}), bf16[128,64,20]{0,2,1:T(8,128)(2,1)S(1)}, u32[]{:S(2)}, u32[]{:S(2)}) %all-to-all-start.4) | async-done | bytes 327712 | tf_op jit(solution)/shard_map/all_to_all | solution.py:80
  112.9 11.0 %all-to-all-start.2 = ((bf16[128,64,20]{0,2,1:T(8,128)(2,1)}), bf16[128,64,20]{0,2,1:T(8,128)(2,1)S(1)}, u32[]{:S(2)}, u32[]{:S(2)}) async-start(bf16[128,64,20]{0,2,1:T(8,128)(2,1)} %rev.7), calls=%async_computation.2 | async-start | bytes 786432 | tf_op jit(solution)/shard_map/all_to_all | solution.py:80
  125.1 0.9 fusion.6
  126.2 9.5 %all-to-all-done.2 = bf16[128,64,20]{0,2,1:T(8,128)(2,1)S(1)} async-done(((bf16[128,64,20]{0,2,1:T(8,128)(2,1)}), bf16[128,64,20]{0,2,1:T(8,128)(2,1)S(1)}, u32[]{:S(2)}, u32[]{:S(2)}) %all-to-all-start.2) | async-done | bytes 327712 | tf_op jit(solution)/shard_map/all_to_all | solution.py:80
  135.8 0.7 copy.66
  136.5 0.8 copy.65
  137.4 0.7 copy.63
  138.8 0.8 copy.62
  (43 shorter events, 5.1 us)
Async XLA Ops:
  0.6 1.8 %copy-start.3 = (bf16[1,128,128]{2,1,0:T(8,128)(2,1)S(1)}, bf16[1,128,128]{2,1,0:T(8,128)(2,1)}, u32[]{:S(2)}) copy-start(bf16[1,128,128]{2,1,0:T(8,128)(2,1)} %param.10) | copy-start | bytes 98308
  1.6 0.7 copy-start.7
  2.7 0.8 copy-start.6
  3.8 12.3 %collective-permute-start = (bf16[128,1024]{1,0:T(8,128)(2,1)S(1)}, bf16[128,1024]{1,0:T(8,128)(2,1)}, u32[]{:S(2)}, u32[]{:S(2)}) collective-permute-start(bf16[128,1024]{1,0:T(8,128)(2,1)S(1)} %copy.49), channel_id=1, source_target_pairs={{0,8},{8,16},{16,24},{24,32},{32,40},{40,48},{48,56},{56,64},{64,7... | collective-permute-start | bytes 786440 | tf_op jit(solution)/shard_map/ppermute | solution.py:14
  16.1 13.0 %copy-start.1 = (bf16[1,128,1024]{2,1,0:T(8,128)(2,1)S(1)}, bf16[1,128,1024]{2,1,0:T(8,128)(2,1)}, u32[]{:S(2)}) copy-start(bf16[1,128,1024]{2,1,0:T(8,128)(2,1)} %param.13) | copy-start | bytes 786436
  16.1 13.0 %copy-start.4 = (bf16[1,128,128]{2,1,0:T(8,128)(2,1)S(1)}, bf16[1,128,128]{2,1,0:T(8,128)(2,1)}, u32[]{:S(2)}) copy-start(bf16[1,128,128]{2,1,0:T(8,128)(2,1)} %param.15) | copy-start | bytes 98308
  16.1 13.0 %copy-start.5 = (bf16[1,128,128]{2,1,0:T(8,128)(2,1)S(1)}, bf16[1,128,128]{2,1,0:T(8,128)(2,1)}, u32[]{:S(2)}) copy-start(bf16[1,128,128]{2,1,0:T(8,128)(2,1)} %param.14) | copy-start | bytes 98308
  16.1 32.2 %all-to-all-start = ((bf16[8,16,1024]{2,1,0:T(8,128)(2,1)}), bf16[8,16,1024]{2,1,0:T(8,128)(2,1)S(1)}, u32[]{:S(2)}, u32[]{:S(2)}) async-start(bf16[8,16,1024]{2,1,0:T(8,128)(2,1)} %bitcast.12), calls=%async_computation | async-start | bytes 524288 | tf_op jit(solution)/shard_map/all_to_all | solution.py:98
  30.2 30.7 %copy-start = (bf16[1,128,1024]{2,1,0:T(8,128)(2,1)S(1)}, bf16[1,128,1024]{2,1,0:T(8,128)(2,1)}, u32[]{:S(2)}) copy-start(bf16[1,128,1024]{2,1,0:T(8,128)(2,1)} %param.9) | copy-start | bytes 786436
  48.3 25.5 %all-to-all-start.3 = ((bf16[128,64,20]{0,2,1:T(8,128)(2,1)}), bf16[128,64,20]{0,2,1:T(8,128)(2,1)S(1)}, u32[]{:S(2)}, u32[]{:S(2)}) async-start(bf16[128,64,20]{0,2,1:T(8,128)(2,1)} %reshape.160), calls=%async_computation.3 | async-start | bytes 786432 | tf_op jit(solution)/shard_map/all_to_all | solution.py:78
  73.8 19.5 %all-to-all-start.1 = ((bf16[128,64,20]{0,2,1:T(8,128)(2,1)}), bf16[128,64,20]{0,2,1:T(8,128)(2,1)S(1)}, u32[]{:S(2)}, u32[]{:S(2)}) async-start(bf16[128,64,20]{0,2,1:T(8,128)(2,1)} %reshape.158), calls=%async_computation.1 | async-start | bytes 786432 | tf_op jit(solution)/shard_map/all_to_all | solution.py:78
  80.6 18.7 %copy-start.2 = (bf16[1,128,1024]{2,1,0:T(8,128)(2,1)S(1)}, bf16[1,128,1024]{2,1,0:T(8,128)(2,1)}, u32[]{:S(2)}) copy-start(bf16[1,128,1024]{2,1,0:T(8,128)(2,1)} %param.17) | copy-start | bytes 786436
  93.3 19.6 %all-to-all-start.4 = ((bf16[128,64,20]{0,2,1:T(8,128)(2,1)}), bf16[128,64,20]{0,2,1:T(8,128)(2,1)S(1)}, u32[]{:S(2)}, u32[]{:S(2)}) async-start(bf16[128,64,20]{0,2,1:T(8,128)(2,1)} %rev.8), calls=%async_computation.4 | async-start | bytes 786432 | tf_op jit(solution)/shard_map/all_to_all | solution.py:80
  99.5 2.4 %copy-start.8 = (s32[1,128]{1,0:T(1,128)S(1)}, s32[1,128]{1,0:T(1,128)}, u32[]{:S(2)}) copy-start(s32[1,128]{1,0:T(1,128)} %param.16) | copy-start | bytes 1540
  99.5 24.9 %collective-permute-start.1 = (bf16[128,1024]{0,1:T(8,128)(2,1)S(1)}, bf16[128,1024]{0,1:T(8,128)(2,1)S(1)}, u32[]{:S(2)}, u32[]{:S(2)}) collective-permute-start(bf16[128,1024]{0,1:T(8,128)(2,1)S(1)} %bitcast.130), channel_id=1, source_target_pairs={{0,504},{8,0},{16,8},{24,16},{32,24},{40,32},{48,40},{56,48},{64,5... | collective-permute-start | bytes 786440 | tf_op jit(solution)/shard_map/ppermute | solution.py:14
  112.9 22.7 %all-to-all-start.2 = ((bf16[128,64,20]{0,2,1:T(8,128)(2,1)}), bf16[128,64,20]{0,2,1:T(8,128)(2,1)S(1)}, u32[]{:S(2)}, u32[]{:S(2)}) async-start(bf16[128,64,20]{0,2,1:T(8,128)(2,1)} %rev.7), calls=%async_computation.2 | async-start | bytes 786432 | tf_op jit(solution)/shard_map/all_to_all | solution.py:80
where the time goes:
time: 140 us
  waiting for transfers between devices  70.1 us (50%)
  starting transfers between devices  54.4 us (39%)
  local copies, waits for them, and re-layouts  11.3 us (8%)
  matrix products  2.33 us (2%)
    all_to_all x2, waiting for transfers between devices, mirror_move(): lax.all_to_all(pieces, 'section', split_axis=1, concat_axis=1, tiled=True)  24.5 us
    all_to_all x2, waiting for transfers between devices, mirror_move(): lax.all_to_all(flipped, 'section', split_axis=1, concat_axis=1, tiled=True)  18.7 us
    all_to_all x2, starting transfers between devices, mirror_move(): lax.all_to_all(pieces, 'section', split_axis=1, concat_axis=1, tiled=True)  18.6 us
    all_to_all x1, waiting for transfers between devices, shards(): lax.all_to_all(shifted, 'tp', split_axis=0, concat_axis=1, tiled=True)  18.1 us
    all_to_all x2, starting transfers between devices, mirror_move(): lax.all_to_all(flipped, 'section', split_axis=1, concat_axis=1, tiled=True)  17 us
    all_to_all x1, starting transfers between devices, shards(): lax.all_to_all(shifted, 'tp', split_axis=0, concat_axis=1, tiled=True)  13 us
    ppermute x2, waiting for transfers between devices, shifted_2(): return lax.ppermute(value, axis, pairs)  8.86 us
    unnamed x25, local copies, waits for them, and re-layouts  6.37 us
  transfers between devices with their start and end apart: 7, of which 6 were waited for; matrix products, arithmetic and copies ran while one was open for 5% of the time, Pallas kernels for 0%

commit v1 on v0

--- a/solution.py
+++ b/solution.py
@@ -71,14 +71,8 @@
 
 
 def mirror_move(stash):
-    section_count = lax.axis_size("section")
-    row_count = stash.shape[0]
-    width = stash.shape[1]
-    pieces = stash.reshape(row_count, section_count, width // section_count)
-    spread = lax.all_to_all(pieces, "section", split_axis=1, concat_axis=1, tiled=True)
-    flipped = jnp.flip(spread, axis=1)
-    collected = lax.all_to_all(flipped, "section", split_axis=1, concat_axis=1, tiled=True)
-    return collected.reshape(row_count, width)
+    count = lax.axis_size("section")
+    return lax.ppermute(stash, "section", [(i, count - 1 - i) for i in range(count)])
 
 
 def shards(fwd_q, fwd_k, fwd_v, fwd_segments, held_q, held_k, held_v, back_segments, up_grad):

time: 140 us -> 69.6 us (0.50)
  the two profiles are of different devices: /device:TPU:2 before, /device:TPU:64 now
where the time goes in v1:
time: 69.6 us; the launch traced here: 69.2 us
  starting transfers between devices  31.4 us (45%)
  waiting for transfers between devices  27.2 us (39%)
  local copies, waits for them, and re-layouts  5.79 us (8%)
  matrix products  2.3 us (3%)
  other arithmetic  1.58 us (2%)
  between operations  0.89 us (1%)
    ppermute x2, waiting for transfers between devices, shifted_2(): return lax.ppermute(value, axis, pairs)  16.2 us
    all_to_all x1, starting transfers between devices, shards(): lax.all_to_all(shifted, 'tp', split_axis=0, concat_axis=1, tiled=True)  13.3 us
    ppermute x2, starting transfers between devices, mirror_move(): lax.ppermute(stash, 'section', [(i, count - 1 - i) for i in range(count)])  12.3 us
    all_to_all x1, waiting for transfers between devices, shards(): lax.all_to_all(shifted, 'tp', split_axis=0, concat_axis=1, tiled=True)  11 us
    ppermute x2, starting transfers between devices, shifted_2(): return lax.ppermute(value, axis, pairs)  5.84 us
    unnamed x16, local copies, waits for them, and re-layouts  3.12 us
  transfers between devices with their start and end apart: 5, of which 2 were waited for; matrix products, arithmetic and copies ran while one was open for 9% of the time, Pallas kernels for 0%

profile of v1, /device:TPU:64, one launch (start us, length us, event | category | flops | bytes accessed | tf_op | source)
XLA Modules:
  0.0 69.2 jit_solution(14924841626843829257)
XLA Ops:
  0.6 1.1 %pad_maximum_fusion.1 = bf16[128,1280]{1,0:T(8,128)(2,1)S(1)} fusion(bf16[128,128]{1,0:T(8,128)(2,1)} %bitcast.122, bf16[128,128]{1,0:T(8,128)(2,1)} %bitcast.123, bf16[128,1024]{1,0:T(8,128)(2,1)} %bitcast.118), kind=kLoop, calls=%fused_computation.24 | loop fusion | flops 983040 | bytes 655360 | tf_op jit(solution)/shard_map/concatenate | solution.py:81
  1.7 6.8 %collective-permute-start.2 = (bf16[128,1280]{1,0:T(8,128)(2,1)S(1)}, bf16[128,1280]{1,0:T(8,128)(2,1)S(1)}, u32[]{:S(2)}, u32[]{:S(2)}) collective-permute-start(bf16[128,1280]{1,0:T(8,128)(2,1)S(1)} %pad_maximum_fusion.1), channel_id=1, source_target_pairs={{0,504},{8,496},{16,488},{24,480},{32,472},{40,464},{48,456},{56,4... | collective-permute-start | bytes 983048 | tf_op jit(solution)/shard_map/ppermute | solution.py:75
  8.5 0.2 copy.47
  8.7 3.7 %collective-permute-start.3 = (bf16[128,1024]{0,1:T(8,128)(2,1)S(1)}, bf16[128,1024]{0,1:T(8,128)(2,1)S(1)}, u32[]{:S(2)}, u32[]{:S(2)}) collective-permute-start(bf16[128,1024]{0,1:T(8,128)(2,1)S(1)} %bitcast.119), channel_id=1, source_target_pairs={{0,504},{8,0},{16,8},{24,16},{32,24},{40,32},{48,40},{56,48},{64,5... | collective-permute-start | bytes 786440 | tf_op jit(solution)/shard_map/ppermute | solution.py:14
  12.5 0.6 copy-done.4
  13.3 0.2 fusion.21
  13.6 0.7 copy-done.3
  14.3 0.3 convolution_convert_fusion.1
  14.7 2.1 %collective-permute-start = (bf16[128,1024]{1,0:T(8,128)(2,1)S(1)}, bf16[128,1024]{1,0:T(8,128)(2,1)}, u32[]{:S(2)}, u32[]{:S(2)}) collective-permute-start(bf16[128,1024]{1,0:T(8,128)(2,1)S(1)} %copy.43), channel_id=1, source_target_pairs={{0,8},{8,16},{16,24},{24,32},{32,40},{40,48},{48,56},{56,64},{64,7... | collective-permute-start | bytes 786440 | tf_op jit(solution)/shard_map/ppermute | solution.py:14
  16.9 5.5 %collective-permute-start.1 = (bf16[128,1280]{1,0:T(8,128)(2,1)S(1)}, bf16[128,1280]{1,0:T(8,128)(2,1)S(1)}, u32[]{:S(2)}, u32[]{:S(2)}) collective-permute-start(bf16[128,1280]{1,0:T(8,128)(2,1)S(1)} %pad_maximum_fusion), channel_id=1, source_target_pairs={{0,504},{8,496},{16,488},{24,480},{32,472},{40,464},{48,456},{56,4... | collective-permute-start | bytes 983048 | tf_op jit(solution)/shard_map/ppermute | solution.py:75
  22.5 16.2 %collective-permute-done = bf16[128,1024]{1,0:T(8,128)(2,1)} collective-permute-done((bf16[128,1024]{1,0:T(8,128)(2,1)S(1)}, bf16[128,1024]{1,0:T(8,128)(2,1)}, u32[]{:S(2)}, u32[]{:S(2)}) %collective-permute-start) | collective-permute-done | bytes 262176 | tf_op jit(solution)/shard_map/ppermute | solution.py:14
  38.7 13.3 %all-to-all-start = ((bf16[8,16,1024]{2,1,0:T(8,128)(2,1)}), bf16[8,16,1024]{2,1,0:T(8,128)(2,1)S(1)}, u32[]{:S(2)}, u32[]{:S(2)}) async-start(bf16[8,16,1024]{2,1,0:T(8,128)(2,1)} %bitcast.12), calls=%async_computation | async-start | bytes 524288 | tf_op jit(solution)/shard_map/all_to_all | solution.py:92
  52.0 0.2 copy.45
  52.2 0.2 fusion.22
  52.5 0.2 multiply_reduce_fusion
  52.9 0.2 fusion.7
  53.1 0.7 %copy.54 = bf16[1,128,128]{2,1,0:T(8,128)(2,1)} copy(bf16[1,128,128]{1,2,0:T(8,128)(2,1)S(1)} %fusion.7) | data formatting | bytes 65536
  53.9 0.2 convolution_convert_fusion
  54.1 0.9 %copy.53 = bf16[1,128,1024]{2,1,0:T(8,128)(2,1)} copy(bf16[1,128,1024]{1,2,0:T(8,128)(2,1)S(1)} %bitcast.117) | data formatting | bytes 524288
  55.0 0.9 %fusion.6 = bf16[1,128,128]{2,1,0:T(8,128)(2,1)} fusion(bf16[128,8,128]{0,2,1:T(8,128)(2,1)S(1)} %bitcast.128, f32[1,8,128,128]{2,3,1,0:T(8,128)S(1)} %get-tuple-element.33, f32[8,128]{1,0:T(8,128)S(1)} %fusion.10, f32[8,128]{1,0:T(8,128)S(1)} %get-tuple-element.32), kind=kOutput, calls=%fused_computation.13 | convolution fusion | flops 33964032 | bytes 827392 | tf_op jit(solution)/shard_map/kgqs,qkgd->skd/dot_general | solution.py:56
  55.8 0.6 slice_bitcast_fusion.4
  56.5 0.7 %slice_bitcast_fusion = bf16[1,128,1024]{2,1,0:T(8,128)(2,1)} fusion(bf16[128,1280]{1,0:T(8,128)(2,1)S(1)} %collective-permute-done.1), kind=kLoop, calls=%fused_computation.26 | loop fusion | bytes 524288 | tf_op jit(solution)/shard_map/broadcast_in_dim | solution.py:98
  57.2 11.0 %all-to-all-done = bf16[8,16,1024]{2,1,0:T(8,128)(2,1)S(1)} async-done(((bf16[8,16,1024]{2,1,0:T(8,128)(2,1)}), bf16[8,16,1024]{2,1,0:T(8,128)(2,1)S(1)}, u32[]{:S(2)}, u32[]{:S(2)}) %all-to-all-start) | async-done | bytes 262176 | tf_op jit(solution)/shard_map/all_to_all | solution.py:92
  68.4 0.8 %broadcast_in_dim.38 = bf16[1,16,8192]{2,1,0:T(8,128)(2,1)} reshape(bf16[16,8,1024]{2,1,0:T(8,128)(2,1)S(1)} %copy.44) | data formatting | bytes 524288 | tf_op jit(solution)/shard_map/broadcast_in_dim | solution.py:97
  (23 shorter events, 0.9 us)
Async XLA Ops:
  0.6 7.9 %copy-start.1 = (bf16[1,128,1024]{2,1,0:T(8,128)(2,1)S(1)}, bf16[1,128,1024]{2,1,0:T(8,128)(2,1)}, u32[]{:S(2)}) copy-start(bf16[1,128,1024]{2,1,0:T(8,128)(2,1)} %param.17) | copy-start | bytes 786436
  1.7 10.7 %copy-start = (bf16[1,128,1024]{2,1,0:T(8,128)(2,1)S(1)}, bf16[1,128,1024]{2,1,0:T(8,128)(2,1)}, u32[]{:S(2)}) copy-start(bf16[1,128,1024]{2,1,0:T(8,128)(2,1)} %param.9) | copy-start | bytes 786436
  1.7 50.2 %collective-permute-start.2 = (bf16[128,1280]{1,0:T(8,128)(2,1)S(1)}, bf16[128,1280]{1,0:T(8,128)(2,1)S(1)}, u32[]{:S(2)}, u32[]{:S(2)}) collective-permute-start(bf16[128,1280]{1,0:T(8,128)(2,1)S(1)} %pad_maximum_fusion.1), channel_id=1, source_target_pairs={{0,504},{8,496},{16,488},{24,480},{32,472},{40,464},{48,456},{56,4... | collective-permute-start | bytes 983048 | tf_op jit(solution)/shard_map/ppermute | solution.py:75
  8.7 43.8 %collective-permute-start.3 = (bf16[128,1024]{0,1:T(8,128)(2,1)S(1)}, bf16[128,1024]{0,1:T(8,128)(2,1)S(1)}, u32[]{:S(2)}, u32[]{:S(2)}) collective-permute-start(bf16[128,1024]{0,1:T(8,128)(2,1)S(1)} %bitcast.119), channel_id=1, source_target_pairs={{0,504},{8,0},{16,8},{24,16},{32,24},{40,32},{48,40},{56,48},{64,5... | collective-permute-start | bytes 786440 | tf_op jit(solution)/shard_map/ppermute | solution.py:14
  12.5 0.8 %copy-start.2 = (bf16[1,128,128]{2,1,0:T(8,128)(2,1)S(1)}, bf16[1,128,128]{2,1,0:T(8,128)(2,1)}, u32[]{:S(2)}) copy-start(bf16[1,128,128]{2,1,0:T(8,128)(2,1)} %param.10) | copy-start | bytes 98308
  12.5 0.7 copy-start.4
  13.5 0.8 %copy-start.3 = (bf16[1,128,128]{2,1,0:T(8,128)(2,1)S(1)}, bf16[1,128,128]{2,1,0:T(8,128)(2,1)}, u32[]{:S(2)}) copy-start(bf16[1,128,128]{2,1,0:T(8,128)(2,1)} %param.11) | copy-start | bytes 98308
  14.7 23.9 %collective-permute-start = (bf16[128,1024]{1,0:T(8,128)(2,1)S(1)}, bf16[128,1024]{1,0:T(8,128)(2,1)}, u32[]{:S(2)}, u32[]{:S(2)}) collective-permute-start(bf16[128,1024]{1,0:T(8,128)(2,1)S(1)} %copy.43), channel_id=1, source_target_pairs={{0,8},{8,16},{16,24},{24,32},{32,40},{40,48},{48,56},{56,64},{64,7... | collective-permute-start | bytes 786440 | tf_op jit(solution)/shard_map/ppermute | solution.py:14
  16.9 5.5 %copy-start.5 = (s32[1,128]{1,0:T(1,128)S(1)}, s32[1,128]{1,0:T(1,128)}, u32[]{:S(2)}) copy-start(s32[1,128]{1,0:T(1,128)} %param.16) | copy-start | bytes 1540
  16.9 39.0 %collective-permute-start.1 = (bf16[128,1280]{1,0:T(8,128)(2,1)S(1)}, bf16[128,1280]{1,0:T(8,128)(2,1)S(1)}, u32[]{:S(2)}, u32[]{:S(2)}) collective-permute-start(bf16[128,1280]{1,0:T(8,128)(2,1)S(1)} %pad_maximum_fusion), channel_id=1, source_target_pairs={{0,504},{8,496},{16,488},{24,480},{32,472},{40,464},{48,456},{56,4... | collective-permute-start | bytes 983048 | tf_op jit(solution)/shard_map/ppermute | solution.py:75
  38.7 29.5 %all-to-all-start = ((bf16[8,16,1024]{2,1,0:T(8,128)(2,1)}), bf16[8,16,1024]{2,1,0:T(8,128)(2,1)S(1)}, u32[]{:S(2)}, u32[]{:S(2)}) async-start(bf16[8,16,1024]{2,1,0:T(8,128)(2,1)} %bitcast.12), calls=%async_computation | async-start | bytes 524288 | tf_op jit(solution)/shard_map/all_to_all | solution.py:92

commit v2 on v1

v2 whole, which is shorter than its diff:
```python
import jax
import jax.numpy as jnp
from jax import lax
from jax.experimental import pallas as pl
from jax.experimental.pallas import tpu as pltpu
from jax.sharding import PartitionSpec as P

HD = 128
SCALE = HD ** -0.5
VMEM = pl.BlockSpec(memory_space=pltpu.VMEM)
FORWARD_FLOPS = 4
BACKWARD_FLOPS = 100


def contract(left, right, left_dim, right_dim):
    return lax.dot_general(left, right, (((left_dim,), (right_dim,)), ((), ())), preferred_element_type=jnp.float32)


def stacked(ref, width):
    return jnp.concatenate([ref[:, start : start + HD] for start in range(0, width, HD)], axis=0)


def unstack(ref, heads):
    rows, width = ref.shape
    for head in range(width // HD):
        ref[:, head * HD : (head + 1) * HD] = heads[head * rows : (head + 1) * rows]


def probability(queries, keys, segments):
    count = segments.shape[1]
    across = jnp.broadcast_to(segments, (count, count))
    key_at = lax.broadcasted_iota(jnp.int32, (count, count), 0)
    query_at = lax.broadcasted_iota(jnp.int32, (count, count), 1)
    allowed = (across == across.T) & (key_at <= query_at)
    allowed = jnp.concatenate([allowed] * (queries.shape[0] // count), axis=1)
    scores = jnp.where(allowed, contract(keys, queries, 1, 1) * SCALE, -jnp.inf)
    weights = jnp.exp(scores - jnp.max(scores, axis=0, keepdims=True))
    return weights * (1.0 / jnp.sum(weights, axis=0, keepdims=True))


def forward_kernel(q_ref, k_ref, v_ref, segments_ref, out_ref):
    prob = probability(stacked(q_ref, q_ref.shape[1]), k_ref[...], segments_ref[...])
    unstack(out_ref, contract(prob.astype(jnp.bfloat16), v_ref[...], 0, 0).astype(jnp.bfloat16))


def backward_kernel(stash_ref, grad_ref, segments_ref, grad_q_ref, grad_k_ref, grad_v_ref):
    width = grad_ref.shape[1]
    queries, grads = stacked(stash_ref, width), stacked(grad_ref, width)
    keys, values = stash_ref[:, width : width + HD], stash_ref[:, width + HD :]
    prob = probability(queries, keys, segments_ref[...])
    dprob = contract(values, grads, 1, 1)
    delta = jnp.sum(prob * dprob, axis=0, keepdims=True)
    dscore = (prob * (dprob - delta) * SCALE).astype(jnp.bfloat16)
    grad_v_ref[...] = contract(prob.astype(jnp.bfloat16), grads, 1, 0).astype(jnp.bfloat16)
    grad_k_ref[...] = contract(dscore, queries, 1, 0).astype(jnp.bfloat16)
    unstack(grad_q_ref, contract(dscore, keys, 0, 0).astype(jnp.bfloat16))


def like(rows, columns):
    return jax.ShapeDtypeStruct((rows, columns), jnp.bfloat16)


def forward(q, k, v, segments):
    rows, width = q.shape
    return pl.pallas_call(
        forward_kernel,
        out_shape=like(rows, width),
        in_specs=[VMEM] * 4,
        out_specs=VMEM,
        cost_estimate=pl.CostEstimate(flops=FORWARD_FLOPS * rows * rows * width, bytes_accessed=8 * rows * width, transcendentals=rows * width),
        name="forward",
    )(q, k, v, segments)


def backward(stash, grad, segments):
    rows, width = grad.shape
    return pl.pallas_call(
        backward_kernel,
        out_shape=(like(rows, width), like(rows, HD), like(rows, HD)),
        in_specs=[VMEM] * 3,
        out_specs=(VMEM, VMEM, VMEM),
        cost_estimate=pl.CostEstimate(flops=BACKWARD_FLOPS * rows * rows * width, bytes_accessed=8 * rows * width, transcendentals=rows * width),
        name="backward",
    )(stash, grad, segments)


def shifted(value, steps):
    count = lax.axis_size("section")
    return lax.ppermute(value, "section", [(i, (i + steps) % count) for i in range(count)])


def mirrored(value):
    count = lax.axis_size("section")
    return lax.ppermute(value, "section", [(i, count - 1 - i) for i in range(count)])


def shards(fwd_q, fwd_k, fwd_v, fwd_segments, held_q, held_k, held_v, back_segments, up_grad):
    width = fwd_q.shape[2]
    held = mirrored(jnp.concatenate([held_q[0], held_k[0], held_v[0]], axis=1))
    out = forward(fwd_q[0], fwd_k[0], fwd_v[0], fwd_segments)
    fresh = mirrored(jnp.concatenate([fwd_q[0], fwd_k[0], fwd_v[0]], axis=1))
    out = shifted(out, 1)
    arriving = shifted(up_grad[0], -1)
    passed = lax.all_to_all(out, "tp", split_axis=0, concat_axis=1, tiled=True)
    grad_q, grad_k, grad_v = backward(held, arriving, back_segments)
    evicted = fresh[:, :width], fresh[:, width : width + HD], fresh[:, width + HD :]
    return tuple(x[None] for x in (passed, *evicted, grad_q, grad_k, grad_v))


def solution(mesh):
    heads, tokens = P("section", None, "tp"), P("section", "tp", None)
    segments = P("section", None)
    in_specs = (heads, heads, heads, segments, heads, heads, heads, segments, heads)
    out_specs = (tokens, heads, heads, heads, heads, heads, heads)
    return jax.shard_map(shards, mesh=mesh, in_specs=in_specs, out_specs=out_specs, check_vma=False)
```

time: 69.6 us -> 66.4 us (0.954)
  the two profiles are of different devices: /device:TPU:64 before, /device:TPU:39 now
where the time goes in v2:
time: 66.4 us; the launch traced here: 66 us
  starting transfers between devices  40.4 us (61%)
  waiting for transfers between devices  16.2 us (24%)
  Pallas kernels  4.74 us (7%)
  local copies, waits for them, and re-layouts  3.78 us (6%)
  between operations  0.82 us (1%)
    ppermute x2, starting transfers between devices, mirrored(): lax.ppermute(value, 'section', [(i, count - 1 - i) for i in range(count)])  19.5 us
    ppermute x2, waiting for transfers between devices, mirrored(): lax.ppermute(value, 'section', [(i, count - 1 - i) for i in range(count)])  16.2 us
    all_to_all x1, starting transfers between devices, shards(): passed = lax.all_to_all(out, 'tp', split_axis=0, concat_axis=1, tiled=True)  14.9 us
    ppermute x2, starting transfers between devices, shifted(): lax.ppermute(value, 'section', [(i, (i + steps) % count) for i in range(c...  5.97 us
    pallas_call x1, Pallas kernels, backward(): pl.pallas_call(backward_kernel, out_shape=(like(rows, width), like(rows,...  2.46 us
    pallas_call x1, Pallas kernels, forward(): pl.pallas_call(forward_kernel, out_shape=like(rows, width), in_specs=[VME...  2.28 us
    broadcast_in_dim x3, local copies, waits for them, and re-layouts, shards(): return tuple((x[None] for x in (passed, *evicted, grad_q, grad_k, grad_v)))  2.18 us
    unnamed x18, local copies, waits for them, and re-layouts  1.45 us
  transfers between devices with their start and end apart: 5, of which 1 were waited for; matrix products, arithmetic and copies ran while one was open for 2% of the time, Pallas kernels for 4%

profile of v2, /device:TPU:39, one launch (start us, length us, event | category | flops | bytes accessed | tf_op | source)
XLA Modules:
  0.0 66.0 jit_solution(3998506776109392991)
XLA Ops:
  0.7 2.3 %forward.1 = bf16[128,1024]{1,0:T(8,128)(2,1)} custom-call(bf16[128,1024]{1,0:T(8,128)(2,1)} %bitcast.19, bf16[128,128]{1,0:T(8,128)(2,1)} %bitcast.22, bf16[128,128]{1,0:T(8,128)(2,1)} %bitcast.24, s32[1,128]{1,0:T(1,128)} %segments_ref.2), custom_call_target="tpu_custom_call" | custom-call | flops 67108864 | bytes 1048576 | tf_op jit(solution)/shard_map/forward/pallas_call | solution.py:65
  2.9 3.4 %collective-permute-start = (bf16[128,1024]{1,0:T(8,128)(2,1)}, bf16[128,1024]{1,0:T(8,128)(2,1)}, u32[]{:S(2)}, u32[]{:S(2)}) collective-permute-start(bf16[128,1024]{1,0:T(8,128)(2,1)} %forward.1), channel_id=1, source_target_pairs={{0,8},{8,16},{16,24},{24,32},{32,40},{40,48},{48,56},{56,64},{64,7... | collective-permute-start | bytes 786440 | tf_op jit(solution)/shard_map/ppermute | solution.py:89
  6.4 0.0 copy-start.7
  6.5 5.7 %collective-permute-start.2 = (bf16[128,1280]{1,0:T(8,128)(2,1)S(1)}, bf16[128,1280]{1,0:T(8,128)(2,1)S(1)}, u32[]{:S(2)}, u32[]{:S(2)}) collective-permute-start(bf16[128,1280]{1,0:T(8,128)(2,1)S(1)} %pad_maximum_fusion.1), channel_id=1, source_target_pairs={{0,504},{8,496},{16,488},{24,480},{32,472},{40,464},{48,456},{56,4... | collective-permute-start | bytes 983048 | tf_op jit(solution)/shard_map/ppermute | solution.py:94
  12.2 2.5 %collective-permute-start.3 = (bf16[128,1024]{1,0:T(8,128)(2,1)S(1)}, bf16[128,1024]{1,0:T(8,128)(2,1)S(1)}, u32[]{:S(2)}, u32[]{:S(2)}) collective-permute-start(bf16[128,1024]{1,0:T(8,128)(2,1)S(1)} %bitcast.28), channel_id=1, source_target_pairs={{0,504},{8,0},{16,8},{24,16},{32,24},{40,32},{48,40},{56,48},{64,5... | collective-permute-start | bytes 786440 | tf_op jit(solution)/shard_map/ppermute | solution.py:89
  14.7 0.0 collective-permute-done
  14.7 0.0 copy-start
  14.7 0.0 copy-start.2
  14.8 0.0 copy-start.3
  14.8 14.9 %all-to-all-start = ((bf16[8,16,1024]{2,1,0:T(8,128)(2,1)}), bf16[8,16,1024]{2,1,0:T(8,128)(2,1)S(1)}, u32[]{:S(2)}, u32[]{:S(2)}) async-start(bf16[8,16,1024]{2,1,0:T(8,128)(2,1)} %bitcast.3), calls=%async_computation | async-start | bytes 524288 | tf_op jit(solution)/shard_map/all_to_all | solution.py:104
  29.7 0.0 copy-done.2
  29.8 13.8 %collective-permute-start.1 = (bf16[128,1280]{1,0:T(8,128)(2,1)S(1)}, bf16[128,1280]{1,0:T(8,128)(2,1)S(1)}, u32[]{:S(2)}, u32[]{:S(2)}) collective-permute-start(bf16[128,1280]{1,0:T(8,128)(2,1)S(1)} %pad_maximum_fusion), channel_id=1, source_target_pairs={{0,504},{8,496},{16,488},{24,480},{32,472},{40,464},{48,456},{56,4... | collective-permute-start | bytes 983048 | tf_op jit(solution)/shard_map/ppermute | solution.py:94
  43.5 0.0 collective-permute-done.3.grad_ref
  43.6 0.0 copy-start.8
  43.6 0.0 collective-permute-done.2.stash_ref
  43.6 0.7 %copy-done.8 = bf16[128,1024]{1,0:T(8,128)(2,1)} copy-done((bf16[128,1024]{1,0:T(8,128)(2,1)}, bf16[128,1024]{1,0:T(8,128)(2,1)S(1)}, u32[]{:S(2)}) %copy-start.8) | copy-done | bytes 262168
  44.3 0.7 %copy-done.6 = bf16[128,1280]{1,0:T(8,128)(2,1)} copy-done((bf16[128,1280]{1,0:T(8,128)(2,1)}, bf16[128,1280]{1,0:T(8,128)(2,1)S(1)}, u32[]{:S(2)}) %copy-start.6) | copy-done | bytes 327704
  45.0 2.5 %backward.1 = (bf16[128,1024]{1,0:T(8,128)(2,1)}, bf16[128,128]{1,0:T(8,128)(2,1)}, bf16[128,128]{1,0:T(8,128)(2,1)}) custom-call(bf16[128,1280]{1,0:T(8,128)(2,1)} %copy-done.6, bf16[128,1024]{1,0:T(8,128)(2,1)} %copy-done.8, s32[1,128]{1,0:T(1,128)} %segments_ref.3), custom_call_target="tpu_custom_call" | custom-call | flops 1677721600 | bytes 1048576 | tf_op jit(solution)/shard_map/backward/pallas_call | solution.py:77
  47.4 16.2 %collective-permute-done.1 = bf16[128,1280]{1,0:T(8,128)(2,1)S(1)} collective-permute-done((bf16[128,1280]{1,0:T(8,128)(2,1)S(1)}, bf16[128,1280]{1,0:T(8,128)(2,1)S(1)}, u32[]{:S(2)}, u32[]{:S(2)}) %collective-permute-start.1) | collective-permute-done | bytes 327712 | tf_op jit(solution)/shard_map/ppermute | solution.py:94
  63.7 0.6 slice_bitcast_fusion.1
  64.3 0.7 %slice_bitcast_fusion = bf16[1,128,1024]{2,1,0:T(8,128)(2,1)} fusion(bf16[128,1280]{1,0:T(8,128)(2,1)S(1)} %collective-permute-done.1), kind=kLoop, calls=%fused_computation.2 | loop fusion | bytes 524288 | tf_op jit(solution)/shard_map/broadcast_in_dim | solution.py:107
  65.0 0.0 all-to-all-done
  65.0 0.1 copy.16
  65.2 0.8 %broadcast_in_dim.21 = bf16[1,16,8192]{2,1,0:T(8,128)(2,1)} reshape(bf16[16,8,1024]{2,1,0:T(8,128)(2,1)S(1)} %copy.16) | data formatting | bytes 524288 | tf_op jit(solution)/shard_map/broadcast_in_dim | solution.py:107
  (12 shorter events, 0.1 us)
Async XLA Ops:
  0.6 5.8 %copy-start.1 = (bf16[1,128,1024]{2,1,0:T(8,128)(2,1)S(1)}, bf16[1,128,1024]{2,1,0:T(8,128)(2,1)}, u32[]{:S(2)}) copy-start(bf16[1,128,1024]{2,1,0:T(8,128)(2,1)} %param.13) | copy-start | bytes 786436
  0.6 5.8 %copy-start.4 = (bf16[1,128,128]{2,1,0:T(8,128)(2,1)S(1)}, bf16[1,128,128]{2,1,0:T(8,128)(2,1)}, u32[]{:S(2)}) copy-start(bf16[1,128,128]{2,1,0:T(8,128)(2,1)} %param.15) | copy-start | bytes 98308
  0.7 5.8 %copy-start.5 = (bf16[1,128,128]{2,1,0:T(8,128)(2,1)S(1)}, bf16[1,128,128]{2,1,0:T(8,128)(2,1)}, u32[]{:S(2)}) copy-start(bf16[1,128,128]{2,1,0:T(8,128)(2,1)} %param.14) | copy-start | bytes 98308
  2.9 11.8 %collective-permute-start = (bf16[128,1024]{1,0:T(8,128)(2,1)}, bf16[128,1024]{1,0:T(8,128)(2,1)}, u32[]{:S(2)}, u32[]{:S(2)}) collective-permute-start(bf16[128,1024]{1,0:T(8,128)(2,1)} %forward.1), channel_id=1, source_target_pairs={{0,8},{8,16},{16,24},{24,32},{32,40},{40,48},{48,56},{56,64},{64,7... | collective-permute-start | bytes 786440 | tf_op jit(solution)/shard_map/ppermute | solution.py:89
  6.4 5.8 %copy-start.7 = (bf16[1,128,1024]{2,1,0:T(8,128)(2,1)S(1)}, bf16[1,128,1024]{2,1,0:T(8,128)(2,1)}, u32[]{:S(2)}) copy-start(bf16[1,128,1024]{2,1,0:T(8,128)(2,1)} %param.17) | copy-start | bytes 786436
  6.5 37.1 %collective-permute-start.2 = (bf16[128,1280]{1,0:T(8,128)(2,1)S(1)}, bf16[128,1280]{1,0:T(8,128)(2,1)S(1)}, u32[]{:S(2)}, u32[]{:S(2)}) collective-permute-start(bf16[128,1280]{1,0:T(8,128)(2,1)S(1)} %pad_maximum_fusion.1), channel_id=1, source_target_pairs={{0,504},{8,496},{16,488},{24,480},{32,472},{40,464},{48,456},{56,4... | collective-permute-start | bytes 983048 | tf_op jit(solution)/shard_map/ppermute | solution.py:94
  12.2 31.4 %collective-permute-start.3 = (bf16[128,1024]{1,0:T(8,128)(2,1)S(1)}, bf16[128,1024]{1,0:T(8,128)(2,1)S(1)}, u32[]{:S(2)}, u32[]{:S(2)}) collective-permute-start(bf16[128,1024]{1,0:T(8,128)(2,1)S(1)} %bitcast.28), channel_id=1, source_target_pairs={{0,504},{8,0},{16,8},{24,16},{32,24},{40,32},{48,40},{56,48},{64,5... | collective-permute-start | bytes 786440 | tf_op jit(solution)/shard_map/ppermute | solution.py:89
  14.7 15.0 %copy-start = (bf16[1,128,1024]{2,1,0:T(8,128)(2,1)S(1)}, bf16[1,128,1024]{2,1,0:T(8,128)(2,1)}, u32[]{:S(2)}) copy-start(bf16[1,128,1024]{2,1,0:T(8,128)(2,1)} %param.9) | copy-start | bytes 786436
  14.7 15.0 %copy-start.2 = (bf16[1,128,128]{2,1,0:T(8,128)(2,1)S(1)}, bf16[1,128,128]{2,1,0:T(8,128)(2,1)}, u32[]{:S(2)}) copy-start(bf16[1,128,128]{2,1,0:T(8,128)(2,1)} %param.10) | copy-start | bytes 98308
  14.8 15.0 %copy-start.3 = (bf16[1,128,128]{2,1,0:T(8,128)(2,1)S(1)}, bf16[1,128,128]{2,1,0:T(8,128)(2,1)}, u32[]{:S(2)}) copy-start(bf16[1,128,128]{2,1,0:T(8,128)(2,1)} %param.11) | copy-start | bytes 98308
  14.8 50.3 %all-to-all-start = ((bf16[8,16,1024]{2,1,0:T(8,128)(2,1)}), bf16[8,16,1024]{2,1,0:T(8,128)(2,1)S(1)}, u32[]{:S(2)}, u32[]{:S(2)}) async-start(bf16[8,16,1024]{2,1,0:T(8,128)(2,1)} %bitcast.3), calls=%async_computation | async-start | bytes 524288 | tf_op jit(solution)/shard_map/all_to_all | solution.py:104
  29.8 33.9 %collective-permute-start.1 = (bf16[128,1280]{1,0:T(8,128)(2,1)S(1)}, bf16[128,1280]{1,0:T(8,128)(2,1)S(1)}, u32[]{:S(2)}, u32[]{:S(2)}) collective-permute-start(bf16[128,1280]{1,0:T(8,128)(2,1)S(1)} %pad_maximum_fusion), channel_id=1, source_target_pairs={{0,504},{8,496},{16,488},{24,480},{32,472},{40,464},{48,456},{56,4... | collective-permute-start | bytes 983048 | tf_op jit(solution)/shard_map/ppermute | solution.py:94
  43.6 0.7 %copy-start.8 = (bf16[128,1024]{1,0:T(8,128)(2,1)}, bf16[128,1024]{1,0:T(8,128)(2,1)S(1)}, u32[]{:S(2)}) copy-start(bf16[128,1024]{1,0:T(8,128)(2,1)S(1)} %collective-permute-done.3.grad_ref) | copy-start | bytes 786436
  44.3 0.7 %copy-start.6 = (bf16[128,1280]{1,0:T(8,128)(2,1)}, bf16[128,1280]{1,0:T(8,128)(2,1)S(1)}, u32[]{:S(2)}) copy-start(bf16[128,1280]{1,0:T(8,128)(2,1)S(1)} %collective-permute-done.2.stash_ref) | copy-start | bytes 983044

commit v3 on v2

--- a/solution.py
+++ b/solution.py
@@ -9,7 +9,7 @@
 SCALE = HD ** -0.5
 VMEM = pl.BlockSpec(memory_space=pltpu.VMEM)
 FORWARD_FLOPS = 4
-BACKWARD_FLOPS = 100
+BACKWARD_FLOPS = 300
 
 
 def contract(left, right, left_dim, right_dim):
@@ -38,15 +38,24 @@
     return weights * (1.0 / jnp.sum(weights, axis=0, keepdims=True))
 
 
-def forward_kernel(q_ref, k_ref, v_ref, segments_ref, out_ref):
-    prob = probability(stacked(q_ref, q_ref.shape[1]), k_ref[...], segments_ref[...])
+def forward_kernel(q_ref, k_ref, v_ref, segments_ref, held_q_ref, held_k_ref, held_v_ref, out_ref, stash_ref):
+    rows, width = q_ref.shape
+    prob = probability(stacked(q_ref, width), k_ref[...], segments_ref[...])
+    stash_ref[:, :width] = held_q_ref[...]
+    stash_ref[:, width : width + HD] = held_k_ref[...]
+    stash_ref[:, width + HD : width + 2 * HD] = held_v_ref[...]
+    whole = width + 2 * HD
+    stash_ref[:, whole : whole + HD] = k_ref[...]
+    stash_ref[:, whole + HD :] = v_ref[...]
     unstack(out_ref, contract(prob.astype(jnp.bfloat16), v_ref[...], 0, 0).astype(jnp.bfloat16))
 
 
-def backward_kernel(stash_ref, grad_ref, segments_ref, grad_q_ref, grad_k_ref, grad_v_ref):
+def backward_kernel(stash_ref, grad_ref, segments_ref, grad_q_ref, grad_k_ref, grad_v_ref, fresh_k_ref, fresh_v_ref):
     width = grad_ref.shape[1]
+    fresh_k_ref[...] = stash_ref[:, width + 2 * HD : width + 3 * HD]
+    fresh_v_ref[...] = stash_ref[:, width + 3 * HD :]
     queries, grads = stacked(stash_ref, width), stacked(grad_ref, width)
-    keys, values = stash_ref[:, width : width + HD], stash_ref[:, width + HD :]
+    keys, values = stash_ref[:, width : width + HD], stash_ref[:, width + HD : width + 2 * HD]
     prob = probability(queries, keys, segments_ref[...])
     dprob = contract(values, grads, 1, 1)
     delta = jnp.sum(prob * dprob, axis=0, keepdims=True)
@@ -60,25 +69,26 @@
     return jax.ShapeDtypeStruct((rows, columns), jnp.bfloat16)
 
 
-def forward(q, k, v, segments):
+def forward(q, k, v, segments, held_q, held_k, held_v):
     rows, width = q.shape
+    whole = width + 2 * HD
     return pl.pallas_call(
         forward_kernel,
-        out_shape=like(rows, width),
-        in_specs=[VMEM] * 4,
-        out_specs=VMEM,
-        cost_estimate=pl.CostEstimate(flops=FORWARD_FLOPS * rows * rows * width, bytes_accessed=8 * rows * width, transcendentals=rows * width),
+        out_shape=(like(rows, width), like(rows, whole + 2 * HD)),
+        in_specs=[VMEM] * 7,
+        out_specs=(VMEM,) * 2,
+        cost_estimate=pl.CostEstimate(flops=FORWARD_FLOPS * rows * rows * width, bytes_accessed=20 * rows * width, transcendentals=rows * width),
         name="forward",
-    )(q, k, v, segments)
+    )(q, k, v, segments, held_q, held_k, held_v)
 
 
 def backward(stash, grad, segments):
     rows, width = grad.shape
     return pl.pallas_call(
         backward_kernel,
-        out_shape=(like(rows, width), like(rows, HD), like(rows, HD)),
+        out_shape=(like(rows, width),) + (like(rows, HD),) * 4,
         in_specs=[VMEM] * 3,
-        out_specs=(VMEM, VMEM, VMEM),
+        out_specs=(VMEM,) * 5,
         cost_estimate=pl.CostEstimate(flops=BACKWARD_FLOPS * rows * rows * width, bytes_accessed=8 * rows * width, transcendentals=rows * width),
         name="backward",
     )(stash, grad, segments)
@@ -89,22 +99,28 @@
     return lax.ppermute(value, "section", [(i, (i + steps) % count) for i in range(count)])
 
 
-def mirrored(value):
-    count = lax.axis_size("section")
-    return lax.ppermute(value, "section", [(i, count - 1 - i) for i in range(count)])
+def mirrored(value, lines=None):
+    count, parts = lax.axis_size("section"), lax.axis_size("tp")
+    if lines is None:
+        return lax.ppermute(value, "section", [(i, count - 1 - i) for i in range(count)])
+    pairs = [(i * parts + t, (count - 1 - i) * parts + t) for i in range(count) for t in range(parts) if t // 2 in lines]
+    return lax.ppermute(value, ("section", "tp"), pairs)
 
 
 def shards(fwd_q, fwd_k, fwd_v, fwd_segments, held_q, held_k, held_v, back_segments, up_grad):
-    width = fwd_q.shape[2]
-    held = mirrored(jnp.concatenate([held_q[0], held_k[0], held_v[0]], axis=1))
-    out = forward(fwd_q[0], fwd_k[0], fwd_v[0], fwd_segments)
-    fresh = mirrored(jnp.concatenate([fwd_q[0], fwd_k[0], fwd_v[0]], axis=1))
+    arriving = shifted(up_grad[0], -1)
+    out, stash = forward(fwd_q[0], fwd_k[0], fwd_v[0], fwd_segments, held_q[0], held_k[0], held_v[0])
     out = shifted(out, 1)
-    arriving = shifted(up_grad[0], -1)
+    stash = mirrored(stash)
+    lines = range(lax.axis_size("tp") // 2)
+    early_q = mirrored(fwd_q[0], lines[:1])
     passed = lax.all_to_all(out, "tp", split_axis=0, concat_axis=1, tiled=True)
-    grad_q, grad_k, grad_v = backward(held, arriving, back_segments)
-    evicted = fresh[:, :width], fresh[:, width : width + HD], fresh[:, width + HD :]
-    return tuple(x[None] for x in (passed, *evicted, grad_q, grad_k, grad_v))
+    late_q = mirrored(fwd_q[0], lines[1:])
+    stash, early_q = lax.optimization_barrier((stash, early_q))
+    grad_q, grad_k, grad_v, evicted_k, evicted_v = backward(stash, arriving, back_segments)
+    late_q, grad_k = lax.optimization_barrier((late_q, grad_k))
+    evicted_q = jnp.where(lax.axis_index("tp") < 2, early_q, late_q)
+    return tuple(x[None] for x in (passed, evicted_q, evicted_k, evicted_v, grad_q, grad_k, grad_v))
 
 
 def solution(mesh):

time: 66.4 us -> 65.9 us (level)
  the two profiles are of different devices: /device:TPU:39 before, /device:TPU:32 now
where the time goes in v3:
time: 65.9 us; the launch traced here: 65.6 us
  starting transfers between devices  30.3 us (46%)
  waiting for transfers between devices  26.5 us (40%)
  Pallas kernels  4.98 us (8%)
  local copies, waits for them, and re-layouts  2.42 us (4%)
  other arithmetic  0.73 us (1%)
  between operations  0.73 us (1%)
    ppermute x2, waiting for transfers between devices, mirrored(): return lax.ppermute(value, ('section', 'tp'), pairs)  26 us
    all_to_all x1, starting transfers between devices, shards(): passed = lax.all_to_all(out, 'tp', split_axis=0, concat_axis=1, tiled=True)  9.79 us
    ppermute x2, starting transfers between devices, shifted(): lax.ppermute(value, 'section', [(i, (i + steps) % count) for i in range(c...  9.07 us
    ppermute x1, starting transfers between devices, mirrored(): lax.ppermute(value, 'section', [(i, count - 1 - i) for i in range(count)])  8.81 us
    ppermute x2, starting transfers between devices, mirrored(): return lax.ppermute(value, ('section', 'tp'), pairs)  2.59 us
    pallas_call x1, Pallas kernels, forward(): pl.pallas_call(forward_kernel, out_shape=(like(rows, width), like(rows, w...  2.5 us
    pallas_call x1, Pallas kernels, backward(): pl.pallas_call(backward_kernel, out_shape=(like(rows, width),) + (like(ro...  2.48 us
    unnamed x8, local copies, waits for them, and re-layouts  1.45 us
  transfers between devices with their start and end apart: 6, of which 2 were waited for; matrix products, arithmetic and copies ran while one was open for 1% of the time, Pallas kernels for 4%

profile of v3, /device:TPU:32, one launch (start us, length us, event | category | flops | bytes accessed | tf_op | source)
XLA Modules:
  0.0 65.6 jit_solution(15694984252794636865)
XLA Ops:
  0.6 0.0 copy-start
  0.6 0.0 copy-start.2
  0.7 2.5 %forward.1 = (bf16[128,1024]{1,0:T(8,128)(2,1)}, bf16[128,1536]{1,0:T(8,128)(2,1)}) custom-call(bf16[128,1024]{1,0:T(8,128)(2,1)} %bitcast.18, bf16[128,128]{1,0:T(8,128)(2,1)} %bitcast.21, bf16[128,128]{1,0:T(8,128)(2,1)} %bitcast.22, s32[1,128]{1,0:T(1,128)} %segments_ref.2, bf16[128,1024]{1,0:T(8,128)(2,1)} %bitcast.17, bf16[128,128]{1,0:T(8,128)(2,1)} %bitcast.23, ...), custom_call_target="tpu_custom_call" | custom-call | flops 67108864 | bytes 2621440 | tf_op jit(solution)/shard_map/forward/pallas_call | solution.py:75
  3.2 3.4 %collective-permute-start = (bf16[128,1024]{1,0:T(8,128)(2,1)}, bf16[128,1024]{1,0:T(8,128)(2,1)}, u32[]{:S(2)}, u32[]{:S(2)}) collective-permute-start(bf16[128,1024]{1,0:T(8,128)(2,1)} %get-tuple-element.18), channel_id=1, source_target_pairs={{0,8},{8,16},{16,24},{24,32},{32,40},{40,48},{48,56},{56,64},{64,7... | collective-permute-start | bytes 786440 | tf_op jit(solution)/shard_map/ppermute | solution.py:99
  6.6 8.8 %collective-permute-start.1 = (bf16[128,1536]{1,0:T(8,128)(2,1)}, bf16[128,1536]{1,0:T(8,128)(2,1)S(1)}, u32[]{:S(2)}, u32[]{:S(2)}) collective-permute-start(bf16[128,1536]{1,0:T(8,128)(2,1)} %get-tuple-element.19), channel_id=1, source_target_pairs={{0,504},{8,496},{16,488},{24,480},{32,472},{40,464},{48,456},{56,4... | collective-permute-start | bytes 1179656 | tf_op jit(solution)/shard_map/ppermute | solution.py:105
  15.4 0.0 copy-done
  15.4 1.9 %collective-permute-start.2 = (bf16[128,1024]{1,0:T(8,128)(2,1)S(1)}, bf16[128,1024]{1,0:T(8,128)(2,1)S(1)}, u32[]{:S(2)}, u32[]{:S(2)}) collective-permute-start(bf16[128,1024]{1,0:T(8,128)(2,1)S(1)} %bitcast.19), channel_id=1, source_target_pairs={{0,504},{1,505},{8,496},{9,497},{16,488},{17,489},{24,480},{25,481... | collective-permute-start | bytes 786440 | tf_op jit(solution)/shard_map/ppermute | solution.py:107
  17.3 0.0 copy-done.2
  17.3 5.7 %collective-permute-start.4 = (bf16[128,1024]{1,0:T(8,128)(2,1)S(1)}, bf16[128,1024]{1,0:T(8,128)(2,1)S(1)}, u32[]{:S(2)}, u32[]{:S(2)}) collective-permute-start(bf16[128,1024]{1,0:T(8,128)(2,1)S(1)} %bitcast.25), channel_id=1, source_target_pairs={{0,504},{8,0},{16,8},{24,16},{32,24},{40,32},{48,40},{56,48},{64,5... | collective-permute-start | bytes 786440 | tf_op jit(solution)/shard_map/ppermute | solution.py:99
  23.0 0.0 collective-permute-done
  23.0 9.8 %all-to-all-start = ((bf16[8,16,1024]{2,1,0:T(8,128)(2,1)}), bf16[8,16,1024]{2,1,0:T(8,128)(2,1)S(1)}, u32[]{:S(2)}, u32[]{:S(2)}) async-start(bf16[8,16,1024]{2,1,0:T(8,128)(2,1)} %bitcast.6), calls=%async_computation | async-start | bytes 524288 | tf_op jit(solution)/shard_map/all_to_all | solution.py:117
  32.8 0.7 %collective-permute-start.3 = (bf16[128,1024]{1,0:T(8,128)(2,1)S(1)}, bf16[128,1024]{1,0:T(8,128)(2,1)S(1)}, u32[]{:S(2)}, u32[]{:S(2)}) collective-permute-start(bf16[128,1024]{1,0:T(8,128)(2,1)S(1)} %bitcast.20), channel_id=1, source_target_pairs={{2,506},{3,507},{4,508},{5,509},{6,510},{7,511},{10,498},{11,499},... | collective-permute-start | bytes 786440 | tf_op jit(solution)/shard_map/ppermute | solution.py:107
  33.5 26.0 %collective-permute-done.2 = bf16[128,1024]{1,0:T(8,128)(2,1)S(1)} collective-permute-done((bf16[128,1024]{1,0:T(8,128)(2,1)S(1)}, bf16[128,1024]{1,0:T(8,128)(2,1)S(1)}, u32[]{:S(2)}, u32[]{:S(2)}) %collective-permute-start.2) | collective-permute-done | bytes 262176 | tf_op jit(solution)/shard_map/ppermute | solution.py:107
  59.5 0.0 collective-permute-done.1.stash_ref
  59.5 0.0 copy-start.1
  59.5 0.0 collective-permute-done.4.grad_ref
  59.5 0.7 %copy-done.1 = bf16[128,1536]{1,0:T(8,128)(2,1)} copy-done((bf16[128,1536]{1,0:T(8,128)(2,1)}, bf16[128,1536]{1,0:T(8,128)(2,1)S(1)}, u32[]{:S(2)}) %copy-start.1) | copy-done | bytes 393240
  60.2 0.7 %copy-done.3 = bf16[128,1024]{1,0:T(8,128)(2,1)} copy-done((bf16[128,1024]{1,0:T(8,128)(2,1)}, bf16[128,1024]{1,0:T(8,128)(2,1)S(1)}, u32[]{:S(2)}) %copy-start.3) | copy-done | bytes 262168
  60.9 2.5 %backward.1 = (bf16[128,1024]{1,0:T(8,128)(2,1)}, bf16[128,128]{1,0:T(8,128)(2,1)}, bf16[128,128]{1,0:T(8,128)(2,1)}, bf16[128,128]{1,0:T(8,128)(2,1)}, bf16[128,128]{1,0:T(8,128)(2,1)}) custom-call(bf16[128,1536]{1,0:T(8,128)(2,1)} %copy-done.1, bf16[128,1024]{1,0:T(8,128)(2,1)} %copy-done.3, s32[1,128]{1,0:T(1,128)} %segments_ref.3), custom_call_target="tpu_custom_call" | custom-call | flops 5033164800 | bytes 1048576 | tf_op jit(solution)/shard_map/backward/pallas_call | solution.py:87
  63.4 0.0 collective-permute-done.3
  63.4 0.7 %select_bitcast_fusion = bf16[1,128,1024]{2,1,0:T(8,128)(2,1)} fusion(bf16[128,1024]{1,0:T(8,128)(2,1)S(1)} %collective-permute-done.2, bf16[128,1024]{1,0:T(8,128)(2,1)S(1)} %collective-permute-done.3, pred[]{:T(512)S(6)} %lt.3), kind=kLoop, calls=%fused_computation | loop fusion | flops 131072 | bytes 786433 | tf_op jit(solution)/shard_map/broadcast_in_dim | solution.py:123
  64.1 0.5 all-to-all-done
  64.6 0.1 copy.16
  64.8 0.8 %broadcast_in_dim.21 = bf16[1,16,8192]{2,1,0:T(8,128)(2,1)} reshape(bf16[16,8,1024]{2,1,0:T(8,128)(2,1)S(1)} %copy.16) | data formatting | bytes 524288 | tf_op jit(solution)/shard_map/broadcast_in_dim | solution.py:123
  (1 shorter events, 0.0 us)
Async XLA Ops:
  0.6 14.7 %copy-start = (bf16[1,128,1024]{2,1,0:T(8,128)(2,1)S(1)}, bf16[1,128,1024]{2,1,0:T(8,128)(2,1)}, u32[]{:S(2)}) copy-start(bf16[1,128,1024]{2,1,0:T(8,128)(2,1)} %param.9) | copy-start | bytes 786436
  0.6 16.7 %copy-start.2 = (bf16[1,128,1024]{2,1,0:T(8,128)(2,1)S(1)}, bf16[1,128,1024]{2,1,0:T(8,128)(2,1)}, u32[]{:S(2)}) copy-start(bf16[1,128,1024]{2,1,0:T(8,128)(2,1)} %param.17) | copy-start | bytes 786436
  3.2 19.9 %collective-permute-start = (bf16[128,1024]{1,0:T(8,128)(2,1)}, bf16[128,1024]{1,0:T(8,128)(2,1)}, u32[]{:S(2)}, u32[]{:S(2)}) collective-permute-start(bf16[128,1024]{1,0:T(8,128)(2,1)} %get-tuple-element.18), channel_id=1, source_target_pairs={{0,8},{8,16},{16,24},{24,32},{32,40},{40,48},{48,56},{56,64},{64,7... | collective-permute-start | bytes 786440 | tf_op jit(solution)/shard_map/ppermute | solution.py:99
  6.6 52.9 %collective-permute-start.1 = (bf16[128,1536]{1,0:T(8,128)(2,1)}, bf16[128,1536]{1,0:T(8,128)(2,1)S(1)}, u32[]{:S(2)}, u32[]{:S(2)}) collective-permute-start(bf16[128,1536]{1,0:T(8,128)(2,1)} %get-tuple-element.19), channel_id=1, source_target_pairs={{0,504},{8,496},{16,488},{24,480},{32,472},{40,464},{48,456},{56,4... | collective-permute-start | bytes 1179656 | tf_op jit(solution)/shard_map/ppermute | solution.py:105
  15.4 44.1 %collective-permute-start.2 = (bf16[128,1024]{1,0:T(8,128)(2,1)S(1)}, bf16[128,1024]{1,0:T(8,128)(2,1)S(1)}, u32[]{:S(2)}, u32[]{:S(2)}) collective-permute-start(bf16[128,1024]{1,0:T(8,128)(2,1)S(1)} %bitcast.19), channel_id=1, source_target_pairs={{0,504},{1,505},{8,496},{9,497},{16,488},{17,489},{24,480},{25,481... | collective-permute-start | bytes 786440 | tf_op jit(solution)/shard_map/ppermute | solution.py:107
  17.3 42.2 %collective-permute-start.4 = (bf16[128,1024]{1,0:T(8,128)(2,1)S(1)}, bf16[128,1024]{1,0:T(8,128)(2,1)S(1)}, u32[]{:S(2)}, u32[]{:S(2)}) collective-permute-start(bf16[128,1024]{1,0:T(8,128)(2,1)S(1)} %bitcast.25), channel_id=1, source_target_pairs={{0,504},{8,0},{16,8},{24,16},{32,24},{40,32},{48,40},{56,48},{64,5... | collective-permute-start | bytes 786440 | tf_op jit(solution)/shard_map/ppermute | solution.py:99
  23.0 41.6 %all-to-all-start = ((bf16[8,16,1024]{2,1,0:T(8,128)(2,1)}), bf16[8,16,1024]{2,1,0:T(8,128)(2,1)S(1)}, u32[]{:S(2)}, u32[]{:S(2)}) async-start(bf16[8,16,1024]{2,1,0:T(8,128)(2,1)} %bitcast.6), calls=%async_computation | async-start | bytes 524288 | tf_op jit(solution)/shard_map/all_to_all | solution.py:117
  32.8 30.6 %collective-permute-start.3 = (bf16[128,1024]{1,0:T(8,128)(2,1)S(1)}, bf16[128,1024]{1,0:T(8,128)(2,1)S(1)}, u32[]{:S(2)}, u32[]{:S(2)}) collective-permute-start(bf16[128,1024]{1,0:T(8,128)(2,1)S(1)} %bitcast.20), channel_id=1, source_target_pairs={{2,506},{3,507},{4,508},{5,509},{6,510},{7,511},{10,498},{11,499},... | collective-permute-start | bytes 786440 | tf_op jit(solution)/shard_map/ppermute | solution.py:107
  59.5 0.7 %copy-start.1 = (bf16[128,1536]{1,0:T(8,128)(2,1)}, bf16[128,1536]{1,0:T(8,128)(2,1)S(1)}, u32[]{:S(2)}) copy-start(bf16[128,1536]{1,0:T(8,128)(2,1)S(1)} %collective-permute-done.1.stash_ref) | copy-start | bytes 1179652
  60.2 0.7 %copy-start.3 = (bf16[128,1024]{1,0:T(8,128)(2,1)}, bf16[128,1024]{1,0:T(8,128)(2,1)S(1)}, u32[]{:S(2)}) copy-start(bf16[128,1024]{1,0:T(8,128)(2,1)S(1)} %collective-permute-done.4.grad_ref) | copy-start | bytes 786436

commit v4 on v3

--- a/solution.py
+++ b/solution.py
@@ -69,12 +69,16 @@
     return jax.ShapeDtypeStruct((rows, columns), jnp.bfloat16)
 
 
+def held_in_vmem(rows, columns):
+    return pltpu.VMEM((rows, columns), jnp.bfloat16)
+
+
 def forward(q, k, v, segments, held_q, held_k, held_v):
     rows, width = q.shape
     whole = width + 2 * HD
     return pl.pallas_call(
         forward_kernel,
-        out_shape=(like(rows, width), like(rows, whole + 2 * HD)),
+        out_shape=(held_in_vmem(rows, width), held_in_vmem(rows, whole + 2 * HD)),
         in_specs=[VMEM] * 7,
         out_specs=(VMEM,) * 2,
         cost_estimate=pl.CostEstimate(flops=FORWARD_FLOPS * rows * rows * width, bytes_accessed=20 * rows * width, transcendentals=rows * width),
@@ -91,7 +95,7 @@
         out_specs=(VMEM,) * 5,
         cost_estimate=pl.CostEstimate(flops=BACKWARD_FLOPS * rows * rows * width, bytes_accessed=8 * rows * width, transcendentals=rows * width),
         name="backward",
-    )(stash, grad, segments)
+    )(pltpu.with_memory_space_constraint(stash, pltpu.VMEM), pltpu.with_memory_space_constraint(grad, pltpu.VMEM), segments)
 
 
 def shifted(value, steps):

time: 65.9 us -> 65 us (0.986)
  waiting for transfers between devices: 26.5 us -> 28.1 us
  local copies, waits for them, and re-layouts: 2.42 us -> 0.98 us
  Pallas kernels: 4.98 us -> 3.81 us
    all_to_all x1, waiting for transfers between devices: 0.47 us -> 2.34 us  [shards(): passed = lax.all_to_all(out, 'tp', split_axis=0, concat_axis=1, tiled=True)]
    unnamed x8 -> x4, local copies, waits for them, and re-layouts: 1.45 us -> 0.01 us
    pallas_call x1, Pallas kernels: 2.5 us -> 1.75 us  [forward(): pl.pallas_call(forward_kernel, out_shape=(held_in_vmem(rows, width), held...]
  transfers between devices with their start and end apart: 6 -> 6, of which waited for: 2 -> 2; matrix products, arithmetic and copies ran while one was open for 1% -> 1% of each run, Pallas kernels for 4% -> 3%
where the time goes in v4:
time: 65 us; the launch traced here: 64.6 us
  starting transfers between devices  30.3 us (47%)
  waiting for transfers between devices  28.1 us (43%)
  Pallas kernels  3.81 us (6%)
  local copies, waits for them, and re-layouts  0.98 us (2%)
  other arithmetic  0.73 us (1%)
  between operations  0.73 us (1%)
    ppermute x2, waiting for transfers between devices, mirrored(): return lax.ppermute(value, ('section', 'tp'), pairs)  25.8 us
    all_to_all x1, starting transfers between devices, shards(): passed = lax.all_to_all(out, 'tp', split_axis=0, concat_axis=1, tiled=True)  9.78 us
    ppermute x2, starting transfers between devices, shifted(): lax.ppermute(value, 'section', [(i, (i + steps) % count) for i in range(c...  9.08 us
    ppermute x1, starting transfers between devices, mirrored(): lax.ppermute(value, 'section', [(i, count - 1 - i) for i in range(count)])  8.81 us
    ppermute x2, starting transfers between devices, mirrored(): return lax.ppermute(value, ('section', 'tp'), pairs)  2.59 us
    all_to_all x1, waiting for transfers between devices, shards(): passed = lax.all_to_all(out, 'tp', split_axis=0, concat_axis=1, tiled=True)  2.34 us
    pallas_call x1, Pallas kernels, backward(): pl.pallas_call(backward_kernel, out_shape=(like(rows, width),) + (like(ro...  2.05 us
    pallas_call x1, Pallas kernels, forward(): pl.pallas_call(forward_kernel, out_shape=(held_in_vmem(rows, width), held...  1.75 us
  transfers between devices with their start and end apart: 6, of which 2 were waited for; matrix products, arithmetic and copies ran while one was open for 1% of the time, Pallas kernels for 3%

profile of v4, /device:TPU:32, one launch (start us, length us, event | category | flops | bytes accessed | tf_op | source)
XLA Modules:
  0.0 64.6 jit_solution(2393334436536478474)
XLA Ops:
  0.6 0.0 copy-start
  0.6 0.0 copy-start.1
  0.7 1.8 %forward.1 = (bf16[128,1024]{1,0:T(8,128)(2,1)S(1)}, bf16[128,1536]{1,0:T(8,128)(2,1)S(1)}) custom-call(bf16[128,1024]{1,0:T(8,128)(2,1)} %bitcast.18, bf16[128,128]{1,0:T(8,128)(2,1)} %bitcast.21, bf16[128,128]{1,0:T(8,128)(2,1)} %bitcast.22, s32[1,128]{1,0:T(1,128)} %segments_ref.2, bf16[128,1024]{1,0:T(8,128)(2,1)} %bitcast.17, ...), custom_call_target="tpu_custom_call" | custom-call | flops 67108864 | bytes 2621440 | tf_op jit(solution)/shard_map/forward/pallas_call | solution.py:79
  2.4 3.4 %collective-permute-start = (bf16[128,1024]{1,0:T(8,128)(2,1)S(1)}, bf16[128,1024]{1,0:T(8,128)(2,1)}, u32[]{:S(2)}, u32[]{:S(2)}) collective-permute-start(bf16[128,1024]{1,0:T(8,128)(2,1)S(1)} %get-tuple-element.18), channel_id=1, source_target_pairs={{0,8},{8,16},{16,24},{24,32},{32,40},{40,48},{48,56},{56,64},{64,7... | collective-permute-start | bytes 786440 | tf_op jit(solution)/shard_map/ppermute | solution.py:103
  5.8 8.8 %collective-permute-start.1 = (bf16[128,1536]{1,0:T(8,128)(2,1)S(1)}, bf16[128,1536]{1,0:T(8,128)(2,1)S(1)}, u32[]{:S(2)}, u32[]{:S(2)}) collective-permute-start(bf16[128,1536]{1,0:T(8,128)(2,1)S(1)} %get-tuple-element.19), channel_id=1, source_target_pairs={{0,504},{8,496},{16,488},{24,480},{32,472},{40,464},{48,456},{56,4... | collective-permute-start | bytes 1179656 | tf_op jit(solution)/shard_map/ppermute | solution.py:109
  14.6 0.0 copy-done
  14.7 1.9 %collective-permute-start.2 = (bf16[128,1024]{1,0:T(8,128)(2,1)S(1)}, bf16[128,1024]{1,0:T(8,128)(2,1)S(1)}, u32[]{:S(2)}, u32[]{:S(2)}) collective-permute-start(bf16[128,1024]{1,0:T(8,128)(2,1)S(1)} %bitcast.19), channel_id=1, source_target_pairs={{0,504},{1,505},{8,496},{9,497},{16,488},{17,489},{24,480},{25,481... | collective-permute-start | bytes 786440 | tf_op jit(solution)/shard_map/ppermute | solution.py:111
  16.6 0.0 copy-done.1
  16.6 5.7 %collective-permute-start.4 = (bf16[128,1024]{1,0:T(8,128)(2,1)S(1)}, bf16[128,1024]{1,0:T(8,128)(2,1)S(1)}, u32[]{:S(2)}, u32[]{:S(2)}) collective-permute-start(bf16[128,1024]{1,0:T(8,128)(2,1)S(1)} %bitcast.25), channel_id=1, source_target_pairs={{0,504},{8,0},{16,8},{24,16},{32,24},{40,32},{48,40},{56,48},{64,5... | collective-permute-start | bytes 786440 | tf_op jit(solution)/shard_map/ppermute | solution.py:103
  22.3 0.0 collective-permute-done
  22.3 9.8 %all-to-all-start = ((bf16[8,16,1024]{2,1,0:T(8,128)(2,1)}), bf16[8,16,1024]{2,1,0:T(8,128)(2,1)S(1)}, u32[]{:S(2)}, u32[]{:S(2)}) async-start(bf16[8,16,1024]{2,1,0:T(8,128)(2,1)} %bitcast.6), calls=%async_computation | async-start | bytes 524288 | tf_op jit(solution)/shard_map/all_to_all | solution.py:121
  32.1 0.7 %collective-permute-start.3 = (bf16[128,1024]{1,0:T(8,128)(2,1)S(1)}, bf16[128,1024]{1,0:T(8,128)(2,1)S(1)}, u32[]{:S(2)}, u32[]{:S(2)}) collective-permute-start(bf16[128,1024]{1,0:T(8,128)(2,1)S(1)} %bitcast.20), channel_id=1, source_target_pairs={{2,506},{3,507},{4,508},{5,509},{6,510},{7,511},{10,498},{11,499},... | collective-permute-start | bytes 786440 | tf_op jit(solution)/shard_map/ppermute | solution.py:111
  32.8 25.8 %collective-permute-done.2 = bf16[128,1024]{1,0:T(8,128)(2,1)S(1)} collective-permute-done((bf16[128,1024]{1,0:T(8,128)(2,1)S(1)}, bf16[128,1024]{1,0:T(8,128)(2,1)S(1)}, u32[]{:S(2)}, u32[]{:S(2)}) %collective-permute-start.2) | collective-permute-done | bytes 262176 | tf_op jit(solution)/shard_map/ppermute | solution.py:111
  58.5 0.0 collective-permute-done.1.stash_ref
  58.5 0.0 collective-permute-done.4.grad_ref
  58.5 2.1 %backward.1 = (bf16[128,1024]{1,0:T(8,128)(2,1)}, bf16[128,128]{1,0:T(8,128)(2,1)}, bf16[128,128]{1,0:T(8,128)(2,1)}, bf16[128,128]{1,0:T(8,128)(2,1)}, bf16[128,128]{1,0:T(8,128)(2,1)}) custom-call(bf16[128,1536]{1,0:T(8,128)(2,1)S(1)} %collective-permute-done.1.stash_ref, bf16[128,1024]{1,0:T(8,128)(2,1)S(1)} %collective-permute-done.4.grad_ref, ...), custom_call_target="tpu_custom_call" | custom-call | flops 5033164800 | bytes 1048576 | tf_op jit(solution)/shard_map/backward/pallas_call | solution.py:91
  60.6 0.0 collective-permute-done.3
  60.6 0.7 %select_bitcast_fusion = bf16[1,128,1024]{2,1,0:T(8,128)(2,1)} fusion(bf16[128,1024]{1,0:T(8,128)(2,1)S(1)} %collective-permute-done.2, bf16[128,1024]{1,0:T(8,128)(2,1)S(1)} %collective-permute-done.3, pred[]{:T(512)S(6)} %lt.3), kind=kLoop, calls=%fused_computation | loop fusion | flops 131072 | bytes 786433 | tf_op jit(solution)/shard_map/broadcast_in_dim | solution.py:127
  61.3 2.3 %all-to-all-done = bf16[8,16,1024]{2,1,0:T(8,128)(2,1)S(1)} async-done(((bf16[8,16,1024]{2,1,0:T(8,128)(2,1)}), bf16[8,16,1024]{2,1,0:T(8,128)(2,1)S(1)}, u32[]{:S(2)}, u32[]{:S(2)}) %all-to-all-start) | async-done | bytes 262176 | tf_op jit(solution)/shard_map/all_to_all | solution.py:121
  63.7 0.1 copy.16
  63.8 0.8 %broadcast_in_dim.21 = bf16[1,16,8192]{2,1,0:T(8,128)(2,1)} reshape(bf16[16,8,1024]{2,1,0:T(8,128)(2,1)S(1)} %copy.16) | data formatting | bytes 524288 | tf_op jit(solution)/shard_map/broadcast_in_dim | solution.py:127
Async XLA Ops:
  0.6 14.0 %copy-start = (bf16[1,128,1024]{2,1,0:T(8,128)(2,1)S(1)}, bf16[1,128,1024]{2,1,0:T(8,128)(2,1)}, u32[]{:S(2)}) copy-start(bf16[1,128,1024]{2,1,0:T(8,128)(2,1)} %param.9) | copy-start | bytes 786436
  0.6 15.9 %copy-start.1 = (bf16[1,128,1024]{2,1,0:T(8,128)(2,1)S(1)}, bf16[1,128,1024]{2,1,0:T(8,128)(2,1)}, u32[]{:S(2)}) copy-start(bf16[1,128,1024]{2,1,0:T(8,128)(2,1)} %param.17) | copy-start | bytes 786436
  2.4 19.9 %collective-permute-start = (bf16[128,1024]{1,0:T(8,128)(2,1)S(1)}, bf16[128,1024]{1,0:T(8,128)(2,1)}, u32[]{:S(2)}, u32[]{:S(2)}) collective-permute-start(bf16[128,1024]{1,0:T(8,128)(2,1)S(1)} %get-tuple-element.18), channel_id=1, source_target_pairs={{0,8},{8,16},{16,24},{24,32},{32,40},{40,48},{48,56},{56,64},{64,7... | collective-permute-start | bytes 786440 | tf_op jit(solution)/shard_map/ppermute | solution.py:103
  5.8 52.7 %collective-permute-start.1 = (bf16[128,1536]{1,0:T(8,128)(2,1)S(1)}, bf16[128,1536]{1,0:T(8,128)(2,1)S(1)}, u32[]{:S(2)}, u32[]{:S(2)}) collective-permute-start(bf16[128,1536]{1,0:T(8,128)(2,1)S(1)} %get-tuple-element.19), channel_id=1, source_target_pairs={{0,504},{8,496},{16,488},{24,480},{32,472},{40,464},{48,456},{56,4... | collective-permute-start | bytes 1179656 | tf_op jit(solution)/shard_map/ppermute | solution.py:109
  14.7 43.9 %collective-permute-start.2 = (bf16[128,1024]{1,0:T(8,128)(2,1)S(1)}, bf16[128,1024]{1,0:T(8,128)(2,1)S(1)}, u32[]{:S(2)}, u32[]{:S(2)}) collective-permute-start(bf16[128,1024]{1,0:T(8,128)(2,1)S(1)} %bitcast.19), channel_id=1, source_target_pairs={{0,504},{1,505},{8,496},{9,497},{16,488},{17,489},{24,480},{25,481... | collective-permute-start | bytes 786440 | tf_op jit(solution)/shard_map/ppermute | solution.py:111
  16.6 41.9 %collective-permute-start.4 = (bf16[128,1024]{1,0:T(8,128)(2,1)S(1)}, bf16[128,1024]{1,0:T(8,128)(2,1)S(1)}, u32[]{:S(2)}, u32[]{:S(2)}) collective-permute-start(bf16[128,1024]{1,0:T(8,128)(2,1)S(1)} %bitcast.25), channel_id=1, source_target_pairs={{0,504},{8,0},{16,8},{24,16},{32,24},{40,32},{48,40},{56,48},{64,5... | collective-permute-start | bytes 786440 | tf_op jit(solution)/shard_map/ppermute | solution.py:103
  22.3 41.4 %all-to-all-start = ((bf16[8,16,1024]{2,1,0:T(8,128)(2,1)}), bf16[8,16,1024]{2,1,0:T(8,128)(2,1)S(1)}, u32[]{:S(2)}, u32[]{:S(2)}) async-start(bf16[8,16,1024]{2,1,0:T(8,128)(2,1)} %bitcast.6), calls=%async_computation | async-start | bytes 524288 | tf_op jit(solution)/shard_map/all_to_all | solution.py:121
  32.1 28.5 %collective-permute-start.3 = (bf16[128,1024]{1,0:T(8,128)(2,1)S(1)}, bf16[128,1024]{1,0:T(8,128)(2,1)S(1)}, u32[]{:S(2)}, u32[]{:S(2)}) collective-permute-start(bf16[128,1024]{1,0:T(8,128)(2,1)S(1)} %bitcast.20), channel_id=1, source_target_pairs={{2,506},{3,507},{4,508},{5,509},{6,510},{7,511},{10,498},{11,499},... | collective-permute-start | bytes 786440 | tf_op jit(solution)/shard_map/ppermute | solution.py:111

commit v5 on v4

--- a/solution.py
+++ b/solution.py
@@ -9,7 +9,7 @@
 SCALE = HD ** -0.5
 VMEM = pl.BlockSpec(memory_space=pltpu.VMEM)
 FORWARD_FLOPS = 4
-BACKWARD_FLOPS = 300
+BACKWARD_FLOPS = 450
 
 
 def contract(left, right, left_dim, right_dim):
@@ -38,24 +38,21 @@
     return weights * (1.0 / jnp.sum(weights, axis=0, keepdims=True))
 
 
-def forward_kernel(q_ref, k_ref, v_ref, segments_ref, held_q_ref, held_k_ref, held_v_ref, out_ref, stash_ref):
+def forward_kernel(q_ref, k_ref, v_ref, segments_ref, held_q_ref, held_k_ref, held_v_ref, out_ref, stash_ref, fresh_ref):
     rows, width = q_ref.shape
     prob = probability(stacked(q_ref, width), k_ref[...], segments_ref[...])
     stash_ref[:, :width] = held_q_ref[...]
     stash_ref[:, width : width + HD] = held_k_ref[...]
-    stash_ref[:, width + HD : width + 2 * HD] = held_v_ref[...]
-    whole = width + 2 * HD
-    stash_ref[:, whole : whole + HD] = k_ref[...]
-    stash_ref[:, whole + HD :] = v_ref[...]
+    stash_ref[:, width + HD :] = held_v_ref[...]
+    fresh_ref[:, :HD] = k_ref[...]
+    fresh_ref[:, HD:] = v_ref[...]
     unstack(out_ref, contract(prob.astype(jnp.bfloat16), v_ref[...], 0, 0).astype(jnp.bfloat16))
 
 
-def backward_kernel(stash_ref, grad_ref, segments_ref, grad_q_ref, grad_k_ref, grad_v_ref, fresh_k_ref, fresh_v_ref):
+def backward_kernel(stash_ref, grad_ref, segments_ref, grad_q_ref, grad_k_ref, grad_v_ref):
     width = grad_ref.shape[1]
-    fresh_k_ref[...] = stash_ref[:, width + 2 * HD : width + 3 * HD]
-    fresh_v_ref[...] = stash_ref[:, width + 3 * HD :]
     queries, grads = stacked(stash_ref, width), stacked(grad_ref, width)
-    keys, values = stash_ref[:, width : width + HD], stash_ref[:, width + HD : width + 2 * HD]
+    keys, values = stash_ref[:, width : width + HD], stash_ref[:, width + HD :]
     prob = probability(queries, keys, segments_ref[...])
     dprob = contract(values, grads, 1, 1)
     delta = jnp.sum(prob * dprob, axis=0, keepdims=True)
@@ -69,6 +66,49 @@
     return jax.ShapeDtypeStruct((rows, columns), jnp.bfloat16)
 
 
+def finish_kernel(pieces_ref, early_ref, late_ref, fresh_ref, passed_ref, q_ref, k_ref, v_ref):
+    parts, _, width = pieces_ref.shape
+    late = jnp.where(lax.rem(lax.axis_index("section"), 16) == 0, parts - 2, 0)
+    for part in range(parts):
+        column = pl.multiple_of(lax.rem(part + late, parts) * width, width)
+        passed_ref[:, pl.ds(column, width)] = pieces_ref[part]
+    k_ref[...] = fresh_ref[:, :HD]
+    v_ref[...] = fresh_ref[:, HD:]
+    is_early = lax.axis_index("tp") < 2
+
+    @pl.when(is_early)
+    def _():
+        q_ref[...] = early_ref[...]
+
+    @pl.when(jnp.logical_not(is_early))
+    def _():
+        q_ref[...] = late_ref[...]
+
+
+def finish(pieces, early, late, fresh):
+    parts, rows, width = pieces.shape
+    tokens = early.shape[0]
+    arrays = (pltpu.with_memory_space_constraint(x, pltpu.VMEM) for x in (pieces, early, late, fresh))
+    return pl.pallas_call(
+        finish_kernel,
+        out_shape=(like(rows, parts * width), like(tokens, width), like(tokens, HD), like(tokens, HD)),
+        in_specs=[VMEM] * 4,
+        out_specs=(VMEM,) * 4,
+        cost_estimate=pl.CostEstimate(flops=0, bytes_accessed=8 * parts * rows * width, transcendentals=0),
+        name="finish",
+    )(*arrays)
+
+
+def handed_on(value):
+    count, parts = lax.axis_size("section"), lax.axis_size("tp")
+    pairs = []
+    for section in range(count):
+        after = (section + 1) % count
+        late = {0: 2}.get(after % 16, 0)
+        pairs += [(section * parts + t, after * parts + (t + late) % parts) for t in range(parts)]
+    return lax.ppermute(value, ("section", "tp"), pairs)
+
+
 def held_in_vmem(rows, columns):
     return pltpu.VMEM((rows, columns), jnp.bfloat16)
 
@@ -78,9 +118,9 @@
     whole = width + 2 * HD
     return pl.pallas_call(
         forward_kernel,
-        out_shape=(held_in_vmem(rows, width), held_in_vmem(rows, whole + 2 * HD)),
+        out_shape=(held_in_vmem(rows, width), held_in_vmem(rows, whole), held_in_vmem(rows, 2 * HD)),
         in_specs=[VMEM] * 7,
-        out_specs=(VMEM,) * 2,
+        out_specs=(VMEM,) * 3,
         cost_estimate=pl.CostEstimate(flops=FORWARD_FLOPS * rows * rows * width, bytes_accessed=20 * rows * width, transcendentals=rows * width),
         name="forward",
     )(q, k, v, segments, held_q, held_k, held_v)
@@ -90,9 +130,9 @@
     rows, width = grad.shape
     return pl.pallas_call(
         backward_kernel,
-        out_shape=(like(rows, width),) + (like(rows, HD),) * 4,
+        out_shape=(like(rows, width),) + (like(rows, HD),) * 2,
         in_specs=[VMEM] * 3,
-        out_specs=(VMEM,) * 5,
+        out_specs=(VMEM,) * 3,
         cost_estimate=pl.CostEstimate(flops=BACKWARD_FLOPS * rows * rows * width, bytes_accessed=8 * rows * width, transcendentals=rows * width),
         name="backward",
     )(pltpu.with_memory_space_constraint(stash, pltpu.VMEM), pltpu.with_memory_space_constraint(grad, pltpu.VMEM), segments)
@@ -113,17 +153,18 @@
 
 def shards(fwd_q, fwd_k, fwd_v, fwd_segments, held_q, held_k, held_v, back_segments, up_grad):
     arriving = shifted(up_grad[0], -1)
-    out, stash = forward(fwd_q[0], fwd_k[0], fwd_v[0], fwd_segments, held_q[0], held_k[0], held_v[0])
-    out = shifted(out, 1)
+    out, stash, fresh = forward(fwd_q[0], fwd_k[0], fwd_v[0], fwd_segments, held_q[0], held_k[0], held_v[0])
+    parts = lax.axis_size("tp")
+    out = handed_on(out).reshape(parts, out.shape[0] // parts, out.shape[1])
     stash = mirrored(stash)
     lines = range(lax.axis_size("tp") // 2)
     early_q = mirrored(fwd_q[0], lines[:1])
-    passed = lax.all_to_all(out, "tp", split_axis=0, concat_axis=1, tiled=True)
+    pieces = lax.all_to_all(out, "tp", split_axis=0, concat_axis=0)
     late_q = mirrored(fwd_q[0], lines[1:])
     stash, early_q = lax.optimization_barrier((stash, early_q))
-    grad_q, grad_k, grad_v, evicted_k, evicted_v = backward(stash, arriving, back_segments)
-    late_q, grad_k = lax.optimization_barrier((late_q, grad_k))
-    evicted_q = jnp.where(lax.axis_index("tp") < 2, early_q, late_q)
+    grad_q, grad_k, grad_v = backward(stash, arriving, back_segments)
+    late_q, fresh, grad_k = lax.optimization_barrier((late_q, mirrored(fresh), grad_k))
+    passed, evicted_q, evicted_k, evicted_v = finish(pieces, early_q, late_q, fresh)
     return tuple(x[None] for x in (passed, evicted_q, evicted_k, evicted_v, grad_q, grad_k, grad_v))
 
 

time: 65 us -> 63 us (0.969)
  waiting for transfers between devices: 28.1 us -> 22.7 us
  starting transfers between devices: 30.3 us -> 34.5 us
  local copies, waits for them, and re-layouts: 0.98 us -> 0.01 us
  Pallas kernels: 3.81 us -> 4.67 us
  other arithmetic: 0.73 us -> 0 us
    ppermute x2, waiting for transfers between devices: 25.8 us -> 20.8 us  [mirrored(): return lax.ppermute(value, ('section', 'tp'), pairs)]
    ppermute x1 -> x2, starting transfers between devices: 8.81 us -> 13.1 us  [mirrored(): lax.ppermute(value, 'section', [(i, count - 1 - i) for i in range(count)])]
    ppermute x2 -> x1, starting transfers between devices: 9.08 us -> 5.68 us  [shifted(): lax.ppermute(value, 'section', [(i, (i + steps) % count) for i in range(c...]
    ppermute x0 -> x1, starting transfers between devices: none -> 3.4 us  [handed_on(): return lax.ppermute(value, ('section', 'tp'), pairs)]
    pallas_call x0 -> x1, Pallas kernels: none -> 0.86 us  [finish(): pl.pallas_call(finish_kernel, out_shape=(like(rows, parts * width), like(...]
    broadcast_in_dim x1 -> x0, local copies, waits for them, and re-layouts: 0.83 us -> none  [shards(): x[None]]
    broadcast_in_dim x1 -> x0, other arithmetic: 0.73 us -> none  [shards(): x[None]]
  transfers between devices with their start and end apart: 6 -> 7, of which waited for: 2 -> 2; matrix products, arithmetic and copies ran while one was open for 1% -> 0% of each run, Pallas kernels for 3% -> 3%
where the time goes in v5:
time: 63 us; the launch traced here: 62.6 us
  starting transfers between devices  34.5 us (55%)
  waiting for transfers between devices  22.7 us (36%)
  Pallas kernels  4.67 us (7%)
  between operations  0.74 us (1%)
    ppermute x2, waiting for transfers between devices, mirrored(): return lax.ppermute(value, ('section', 'tp'), pairs)  20.8 us
    ppermute x2, starting transfers between devices, mirrored(): lax.ppermute(value, 'section', [(i, count - 1 - i) for i in range(count)])  13.1 us
    all_to_all x1, starting transfers between devices, shards(): pieces = lax.all_to_all(out, 'tp', split_axis=0, concat_axis=0)  9.78 us
    ppermute x1, starting transfers between devices, shifted(): lax.ppermute(value, 'section', [(i, (i + steps) % count) for i in range(c...  5.68 us
    ppermute x1, starting transfers between devices, handed_on(): return lax.ppermute(value, ('section', 'tp'), pairs)  3.4 us
    ppermute x2, starting transfers between devices, mirrored(): return lax.ppermute(value, ('section', 'tp'), pairs)  2.59 us
    pallas_call x1, Pallas kernels, backward(): pl.pallas_call(backward_kernel, out_shape=(like(rows, width),) + (like(ro...  2.06 us
    all_to_all x1, waiting for transfers between devices, shards(): pieces = lax.all_to_all(out, 'tp', split_axis=0, concat_axis=0)  1.86 us
  transfers between devices with their start and end apart: 7, of which 2 were waited for; matrix products, arithmetic and copies ran while one was open for 0% of the time, Pallas kernels for 3%

profile of v5, /device:TPU:32, one launch (start us, length us, event | category | flops | bytes accessed | tf_op | source)
XLA Modules:
  0.0 62.6 jit_solution(5022379062811554621)
XLA Ops:
  0.6 0.0 copy-start
  0.6 0.0 copy-start.1
  0.7 1.8 %forward.1 = (bf16[128,1024]{1,0:T(8,128)(2,1)S(1)}, bf16[128,1280]{1,0:T(8,128)(2,1)S(1)}, bf16[128,256]{1,0:T(8,128)(2,1)S(1)}) custom-call(bf16[128,1024]{1,0:T(8,128)(2,1)} %bitcast.16, bf16[128,128]{1,0:T(8,128)(2,1)} %bitcast.19, bf16[128,128]{1,0:T(8,128)(2,1)} %bitcast.20, s32[1,128]{1,0:T(1,128)} %segments_ref.2, bf16[128,1024]{1,0:T(8,128)(2,1)} %bitcast.15, ...), custom_call_target="tpu_custom_call" | custom-call | flops 67108864 | bytes 2621440 | tf_op jit(solution)/shard_map/forward/pallas_call | solution.py:119
  2.4 3.4 %collective-permute-start = (bf16[128,1024]{1,0:T(8,128)(2,1)S(1)}, bf16[128,1024]{1,0:T(8,128)(2,1)}, u32[]{:S(2)}, u32[]{:S(2)}) collective-permute-start(bf16[128,1024]{1,0:T(8,128)(2,1)S(1)} %get-tuple-element.22), channel_id=1, source_target_pairs={{0,8},{1,9},{2,10},{3,11},{4,12},{5,13},{6,14},{7,15},{8,16},{9,17... | collective-permute-start | bytes 786440 | tf_op jit(solution)/shard_map/ppermute | solution.py:109
  5.8 8.8 %collective-permute-start.1 = (bf16[128,1280]{1,0:T(8,128)(2,1)S(1)}, bf16[128,1280]{1,0:T(8,128)(2,1)S(1)}, u32[]{:S(2)}, u32[]{:S(2)}) collective-permute-start(bf16[128,1280]{1,0:T(8,128)(2,1)S(1)} %get-tuple-element.23), channel_id=1, source_target_pairs={{0,504},{8,496},{16,488},{24,480},{32,472},{40,464},{48,456},{56,4... | collective-permute-start | bytes 983048 | tf_op jit(solution)/shard_map/ppermute | solution.py:149
  14.6 0.0 copy-done
  14.7 1.9 %collective-permute-start.2 = (bf16[128,1024]{1,0:T(8,128)(2,1)S(1)}, bf16[128,1024]{1,0:T(8,128)(2,1)S(1)}, u32[]{:S(2)}, u32[]{:S(2)}) collective-permute-start(bf16[128,1024]{1,0:T(8,128)(2,1)S(1)} %bitcast.17), channel_id=1, source_target_pairs={{0,504},{1,505},{8,496},{9,497},{16,488},{17,489},{24,480},{25,481... | collective-permute-start | bytes 786440 | tf_op jit(solution)/shard_map/ppermute | solution.py:151
  16.6 0.0 copy-done.1
  16.6 5.7 %collective-permute-start.5 = (bf16[128,1024]{1,0:T(8,128)(2,1)S(1)}, bf16[128,1024]{1,0:T(8,128)(2,1)S(1)}, u32[]{:S(2)}, u32[]{:S(2)}) collective-permute-start(bf16[128,1024]{1,0:T(8,128)(2,1)S(1)} %bitcast.23), channel_id=1, source_target_pairs={{0,504},{8,0},{16,8},{24,16},{32,24},{40,32},{48,40},{56,48},{64,5... | collective-permute-start | bytes 786440 | tf_op jit(solution)/shard_map/ppermute | solution.py:143
  22.3 0.0 collective-permute-done
  22.3 9.8 %all-to-all-start = ((bf16[8,16,1024]{2,1,0:T(8,128)(2,1)}), bf16[8,16,1024]{2,1,0:T(8,128)(2,1)S(1)}, u32[]{:S(2)}, u32[]{:S(2)}) async-start(bf16[8,16,1024]{2,1,0:T(8,128)(2,1)} %bitcast.6), calls=%async_computation | async-start | bytes 524288 | tf_op jit(solution)/shard_map/all_to_all | solution.py:162
  32.1 0.7 %collective-permute-start.3 = (bf16[128,1024]{1,0:T(8,128)(2,1)S(1)}, bf16[128,1024]{1,0:T(8,128)(2,1)S(1)}, u32[]{:S(2)}, u32[]{:S(2)}) collective-permute-start(bf16[128,1024]{1,0:T(8,128)(2,1)S(1)} %bitcast.18), channel_id=1, source_target_pairs={{2,506},{3,507},{4,508},{5,509},{6,510},{7,511},{10,498},{11,499},... | collective-permute-start | bytes 786440 | tf_op jit(solution)/shard_map/ppermute | solution.py:151
  32.7 4.2 %collective-permute-start.4 = (bf16[128,256]{1,0:T(8,128)(2,1)S(1)}, bf16[128,256]{1,0:T(8,128)(2,1)S(1)}, u32[]{:S(2)}, u32[]{:S(2)}) collective-permute-start(bf16[128,256]{1,0:T(8,128)(2,1)S(1)} %get-tuple-element.25), channel_id=1, source_target_pairs={{0,504},{8,496},{16,488},{24,480},{32,472},{40,464},{48,456},{56,4... | collective-permute-start | bytes 196616 | tf_op jit(solution)/shard_map/ppermute | solution.py:149
  37.0 20.8 %collective-permute-done.2.early_ref = bf16[128,1024]{1,0:T(8,128)(2,1)S(1)} collective-permute-done((bf16[128,1024]{1,0:T(8,128)(2,1)S(1)}, bf16[128,1024]{1,0:T(8,128)(2,1)S(1)}, u32[]{:S(2)}, u32[]{:S(2)}) %collective-permute-start.2) | collective-permute-done | bytes 262176 | tf_op jit(solution)/shard_map/ppermute | solution.py:151
  57.8 0.0 collective-permute-done.1.stash_ref
  57.8 0.0 collective-permute-done.5.grad_ref
  57.8 2.1 %backward.1 = (bf16[128,1024]{1,0:T(8,128)(2,1)}, bf16[128,128]{1,0:T(8,128)(2,1)}, bf16[128,128]{1,0:T(8,128)(2,1)}) custom-call(bf16[128,1280]{1,0:T(8,128)(2,1)S(1)} %collective-permute-done.1.stash_ref, bf16[128,1024]{1,0:T(8,128)(2,1)S(1)} %collective-permute-done.5.grad_ref, s32[1,128]{1,0:T(1,128)} %segments_ref.3), custom_call_target="tpu_custom_call" | custom-call | flops 7549747200 | bytes 1048576 | tf_op jit(solution)/shard_map/backward/pallas_call | solution.py:131
  59.9 0.0 collective-permute-done.4.fresh_ref
  59.9 0.0 collective-permute-done.3.late_ref
  59.9 1.9 %all-to-all-done.pieces_ref = bf16[8,16,1024]{2,1,0:T(8,128)(2,1)S(1)} async-done(((bf16[8,16,1024]{2,1,0:T(8,128)(2,1)}), bf16[8,16,1024]{2,1,0:T(8,128)(2,1)S(1)}, u32[]{:S(2)}, u32[]{:S(2)}) %all-to-all-start) | async-done | bytes 262176 | tf_op jit(solution)/shard_map/all_to_all | solution.py:162
  61.8 0.9 %finish.1 = (bf16[16,8192]{1,0:T(8,128)(2,1)}, bf16[128,1024]{1,0:T(8,128)(2,1)}, bf16[128,128]{1,0:T(8,128)(2,1)}, bf16[128,128]{1,0:T(8,128)(2,1)}) custom-call(bf16[8,16,1024]{2,1,0:T(8,128)(2,1)S(1)} %all-to-all-done.pieces_ref, bf16[128,1024]{1,0:T(8,128)(2,1)S(1)} %collective-permute-done.2.early_ref, ...), custom_call_target="tpu_custom_call" | custom-call | bytes 1048576 | tf_op jit(solution)/shard_map/finish/pallas_call | solution.py:92
Async XLA Ops:
  0.6 14.0 %copy-start = (bf16[1,128,1024]{2,1,0:T(8,128)(2,1)S(1)}, bf16[1,128,1024]{2,1,0:T(8,128)(2,1)}, u32[]{:S(2)}) copy-start(bf16[1,128,1024]{2,1,0:T(8,128)(2,1)} %param.9) | copy-start | bytes 786436
  0.6 15.9 %copy-start.1 = (bf16[1,128,1024]{2,1,0:T(8,128)(2,1)S(1)}, bf16[1,128,1024]{2,1,0:T(8,128)(2,1)}, u32[]{:S(2)}) copy-start(bf16[1,128,1024]{2,1,0:T(8,128)(2,1)} %param.17) | copy-start | bytes 786436
  2.4 19.9 %collective-permute-start = (bf16[128,1024]{1,0:T(8,128)(2,1)S(1)}, bf16[128,1024]{1,0:T(8,128)(2,1)}, u32[]{:S(2)}, u32[]{:S(2)}) collective-permute-start(bf16[128,1024]{1,0:T(8,128)(2,1)S(1)} %get-tuple-element.22), channel_id=1, source_target_pairs={{0,8},{1,9},{2,10},{3,11},{4,12},{5,13},{6,14},{7,15},{8,16},{9,17... | collective-permute-start | bytes 786440 | tf_op jit(solution)/shard_map/ppermute | solution.py:109
  5.8 52.0 %collective-permute-start.1 = (bf16[128,1280]{1,0:T(8,128)(2,1)S(1)}, bf16[128,1280]{1,0:T(8,128)(2,1)S(1)}, u32[]{:S(2)}, u32[]{:S(2)}) collective-permute-start(bf16[128,1280]{1,0:T(8,128)(2,1)S(1)} %get-tuple-element.23), channel_id=1, source_target_pairs={{0,504},{8,496},{16,488},{24,480},{32,472},{40,464},{48,456},{56,4... | collective-permute-start | bytes 983048 | tf_op jit(solution)/shard_map/ppermute | solution.py:149
  14.7 43.2 %collective-permute-start.2 = (bf16[128,1024]{1,0:T(8,128)(2,1)S(1)}, bf16[128,1024]{1,0:T(8,128)(2,1)S(1)}, u32[]{:S(2)}, u32[]{:S(2)}) collective-permute-start(bf16[128,1024]{1,0:T(8,128)(2,1)S(1)} %bitcast.17), channel_id=1, source_target_pairs={{0,504},{1,505},{8,496},{9,497},{16,488},{17,489},{24,480},{25,481... | collective-permute-start | bytes 786440 | tf_op jit(solution)/shard_map/ppermute | solution.py:151
  16.6 41.2 %collective-permute-start.5 = (bf16[128,1024]{1,0:T(8,128)(2,1)S(1)}, bf16[128,1024]{1,0:T(8,128)(2,1)S(1)}, u32[]{:S(2)}, u32[]{:S(2)}) collective-permute-start(bf16[128,1024]{1,0:T(8,128)(2,1)S(1)} %bitcast.23), channel_id=1, source_target_pairs={{0,504},{8,0},{16,8},{24,16},{32,24},{40,32},{48,40},{56,48},{64,5... | collective-permute-start | bytes 786440 | tf_op jit(solution)/shard_map/ppermute | solution.py:143
  22.3 39.5 %all-to-all-start = ((bf16[8,16,1024]{2,1,0:T(8,128)(2,1)}), bf16[8,16,1024]{2,1,0:T(8,128)(2,1)S(1)}, u32[]{:S(2)}, u32[]{:S(2)}) async-start(bf16[8,16,1024]{2,1,0:T(8,128)(2,1)} %bitcast.6), calls=%async_computation | async-start | bytes 524288 | tf_op jit(solution)/shard_map/all_to_all | solution.py:162
  32.1 27.8 %collective-permute-start.3 = (bf16[128,1024]{1,0:T(8,128)(2,1)S(1)}, bf16[128,1024]{1,0:T(8,128)(2,1)S(1)}, u32[]{:S(2)}, u32[]{:S(2)}) collective-permute-start(bf16[128,1024]{1,0:T(8,128)(2,1)S(1)} %bitcast.18), channel_id=1, source_target_pairs={{2,506},{3,507},{4,508},{5,509},{6,510},{7,511},{10,498},{11,499},... | collective-permute-start | bytes 786440 | tf_op jit(solution)/shard_map/ppermute | solution.py:151
  32.7 27.2 %collective-permute-start.4 = (bf16[128,256]{1,0:T(8,128)(2,1)S(1)}, bf16[128,256]{1,0:T(8,128)(2,1)S(1)}, u32[]{:S(2)}, u32[]{:S(2)}) collective-permute-start(bf16[128,256]{1,0:T(8,128)(2,1)S(1)} %get-tuple-element.25), channel_id=1, source_target_pairs={{0,504},{8,496},{16,488},{24,480},{32,472},{40,464},{48,456},{56,4... | collective-permute-start | bytes 196616 | tf_op jit(solution)/shard_map/ppermute | solution.py:149

commit v6 on v5

--- a/solution.py
+++ b/solution.py
@@ -38,15 +38,20 @@
     return weights * (1.0 / jnp.sum(weights, axis=0, keepdims=True))
 
 
-def forward_kernel(q_ref, k_ref, v_ref, segments_ref, held_q_ref, held_k_ref, held_v_ref, out_ref, stash_ref, fresh_ref):
+def forward_kernel(q_ref, k_ref, v_ref, segments_ref, held_q_ref, held_k_ref, held_v_ref, out_ref, stash_ref, fresh_ref, semaphores):
     rows, width = q_ref.shape
+    copies, start = [], 0
+    for index, source in enumerate((held_q_ref, held_k_ref, held_v_ref)):
+        target = stash_ref.at[:, pl.ds(start, source.shape[1])]
+        copies.append(pltpu.make_async_copy(source, target, semaphores.at[index]))
+        copies[-1].start()
+        start = start + source.shape[1]
     prob = probability(stacked(q_ref, width), k_ref[...], segments_ref[...])
-    stash_ref[:, :width] = held_q_ref[...]
-    stash_ref[:, width : width + HD] = held_k_ref[...]
-    stash_ref[:, width + HD :] = held_v_ref[...]
     fresh_ref[:, :HD] = k_ref[...]
     fresh_ref[:, HD:] = v_ref[...]
     unstack(out_ref, contract(prob.astype(jnp.bfloat16), v_ref[...], 0, 0).astype(jnp.bfloat16))
+    for copy in copies:
+        copy.wait()
 
 
 def backward_kernel(stash_ref, grad_ref, segments_ref, grad_q_ref, grad_k_ref, grad_v_ref):
@@ -119,8 +124,9 @@
     return pl.pallas_call(
         forward_kernel,
         out_shape=(held_in_vmem(rows, width), held_in_vmem(rows, whole), held_in_vmem(rows, 2 * HD)),
-        in_specs=[VMEM] * 7,
+        in_specs=[VMEM] * 4 + [pl.BlockSpec(memory_space=pl.ANY)] * 3,
         out_specs=(VMEM,) * 3,
+        scratch_shapes=[pltpu.SemaphoreType.DMA((3,))],
         cost_estimate=pl.CostEstimate(flops=FORWARD_FLOPS * rows * rows * width, bytes_accessed=20 * rows * width, transcendentals=rows * width),
         name="forward",
     )(q, k, v, segments, held_q, held_k, held_v)

time: 63 us -> 63.3 us (level)
  no operation moved by 1% of the time
where the time goes in v6:
time: 63.3 us; the launch traced here: 62.9 us
  starting transfers between devices  34.5 us (55%)
  waiting for transfers between devices  22.7 us (36%)
  Pallas kernels  4.96 us (8%)
  between operations  0.74 us (1%)
    ppermute x2, waiting for transfers between devices, mirrored(): return lax.ppermute(value, ('section', 'tp'), pairs)  20.8 us
    ppermute x2, starting transfers between devices, mirrored(): lax.ppermute(value, 'section', [(i, count - 1 - i) for i in range(count)])  13.1 us
    all_to_all x1, starting transfers between devices, shards(): pieces = lax.all_to_all(out, 'tp', split_axis=0, concat_axis=0)  9.78 us
    ppermute x1, starting transfers between devices, shifted(): lax.ppermute(value, 'section', [(i, (i + steps) % count) for i in range(c...  5.68 us
    ppermute x1, starting transfers between devices, handed_on(): return lax.ppermute(value, ('section', 'tp'), pairs)  3.4 us
    ppermute x2, starting transfers between devices, mirrored(): return lax.ppermute(value, ('section', 'tp'), pairs)  2.59 us
    pallas_call x1, Pallas kernels, backward(): pl.pallas_call(backward_kernel, out_shape=(like(rows, width),) + (like(ro...  2.06 us
    pallas_call x1, Pallas kernels, forward(): pl.pallas_call(forward_kernel, out_shape=(held_in_vmem(rows, width), held...  2.04 us
  transfers between devices with their start and end apart: 7, of which 2 were waited for; matrix products, arithmetic and copies ran while one was open for 0% of the time, Pallas kernels for 3%

profile of v6, /device:TPU:32, one launch (start us, length us, event | category | flops | bytes accessed | tf_op | source)
XLA Modules:
  0.0 62.9 jit_solution(11093863027638981049)
XLA Ops:
  0.6 0.0 copy-start
  0.6 0.0 copy-start.1
  0.7 2.0 %forward.1 = (bf16[128,1024]{1,0:T(8,128)(2,1)S(1)}, bf16[128,1280]{1,0:T(8,128)(2,1)S(1)}, bf16[128,256]{1,0:T(8,128)(2,1)S(1)}) custom-call(bf16[128,1024]{1,0:T(8,128)(2,1)} %bitcast.16, bf16[128,128]{1,0:T(8,128)(2,1)} %bitcast.19, bf16[128,128]{1,0:T(8,128)(2,1)} %bitcast.20, s32[1,128]{1,0:T(1,128)} %segments_ref.2, bf16[128,1024]{1,0:T(8,128)(2,1)} %bitcast.15, ...), custom_call_target="tpu_custom_call" | custom-call | flops 67108864 | bytes 2621440 | tf_op jit(solution)/shard_map/forward/pallas_call | solution.py:124
  2.7 3.4 %collective-permute-start = (bf16[128,1024]{1,0:T(8,128)(2,1)S(1)}, bf16[128,1024]{1,0:T(8,128)(2,1)}, u32[]{:S(2)}, u32[]{:S(2)}) collective-permute-start(bf16[128,1024]{1,0:T(8,128)(2,1)S(1)} %get-tuple-element.22), channel_id=1, source_target_pairs={{0,8},{1,9},{2,10},{3,11},{4,12},{5,13},{6,14},{7,15},{8,16},{9,17... | collective-permute-start | bytes 786440 | tf_op jit(solution)/shard_map/ppermute | solution.py:114
  6.1 8.8 %collective-permute-start.1 = (bf16[128,1280]{1,0:T(8,128)(2,1)S(1)}, bf16[128,1280]{1,0:T(8,128)(2,1)S(1)}, u32[]{:S(2)}, u32[]{:S(2)}) collective-permute-start(bf16[128,1280]{1,0:T(8,128)(2,1)S(1)} %get-tuple-element.23), channel_id=1, source_target_pairs={{0,504},{8,496},{16,488},{24,480},{32,472},{40,464},{48,456},{56,4... | collective-permute-start | bytes 983048 | tf_op jit(solution)/shard_map/ppermute | solution.py:155
  14.9 0.0 copy-done
  14.9 1.9 %collective-permute-start.2 = (bf16[128,1024]{1,0:T(8,128)(2,1)S(1)}, bf16[128,1024]{1,0:T(8,128)(2,1)S(1)}, u32[]{:S(2)}, u32[]{:S(2)}) collective-permute-start(bf16[128,1024]{1,0:T(8,128)(2,1)S(1)} %bitcast.17), channel_id=1, source_target_pairs={{0,504},{1,505},{8,496},{9,497},{16,488},{17,489},{24,480},{25,481... | collective-permute-start | bytes 786440 | tf_op jit(solution)/shard_map/ppermute | solution.py:157
  16.9 0.0 copy-done.1
  16.9 5.7 %collective-permute-start.5 = (bf16[128,1024]{1,0:T(8,128)(2,1)S(1)}, bf16[128,1024]{1,0:T(8,128)(2,1)S(1)}, u32[]{:S(2)}, u32[]{:S(2)}) collective-permute-start(bf16[128,1024]{1,0:T(8,128)(2,1)S(1)} %bitcast.23), channel_id=1, source_target_pairs={{0,504},{8,0},{16,8},{24,16},{32,24},{40,32},{48,40},{56,48},{64,5... | collective-permute-start | bytes 786440 | tf_op jit(solution)/shard_map/ppermute | solution.py:149
  22.6 0.0 collective-permute-done
  22.6 9.8 %all-to-all-start = ((bf16[8,16,1024]{2,1,0:T(8,128)(2,1)}), bf16[8,16,1024]{2,1,0:T(8,128)(2,1)S(1)}, u32[]{:S(2)}, u32[]{:S(2)}) async-start(bf16[8,16,1024]{2,1,0:T(8,128)(2,1)} %bitcast.6), calls=%async_computation | async-start | bytes 524288 | tf_op jit(solution)/shard_map/all_to_all | solution.py:168
  32.4 0.7 %collective-permute-start.3 = (bf16[128,1024]{1,0:T(8,128)(2,1)S(1)}, bf16[128,1024]{1,0:T(8,128)(2,1)S(1)}, u32[]{:S(2)}, u32[]{:S(2)}) collective-permute-start(bf16[128,1024]{1,0:T(8,128)(2,1)S(1)} %bitcast.18), channel_id=1, source_target_pairs={{2,506},{3,507},{4,508},{5,509},{6,510},{7,511},{10,498},{11,499},... | collective-permute-start | bytes 786440 | tf_op jit(solution)/shard_map/ppermute | solution.py:157
  33.0 4.2 %collective-permute-start.4 = (bf16[128,256]{1,0:T(8,128)(2,1)S(1)}, bf16[128,256]{1,0:T(8,128)(2,1)S(1)}, u32[]{:S(2)}, u32[]{:S(2)}) collective-permute-start(bf16[128,256]{1,0:T(8,128)(2,1)S(1)} %get-tuple-element.25), channel_id=1, source_target_pairs={{0,504},{8,496},{16,488},{24,480},{32,472},{40,464},{48,456},{56,4... | collective-permute-start | bytes 196616 | tf_op jit(solution)/shard_map/ppermute | solution.py:155
  37.3 20.8 %collective-permute-done.2.early_ref = bf16[128,1024]{1,0:T(8,128)(2,1)S(1)} collective-permute-done((bf16[128,1024]{1,0:T(8,128)(2,1)S(1)}, bf16[128,1024]{1,0:T(8,128)(2,1)S(1)}, u32[]{:S(2)}, u32[]{:S(2)}) %collective-permute-start.2) | collective-permute-done | bytes 262176 | tf_op jit(solution)/shard_map/ppermute | solution.py:157
  58.1 0.0 collective-permute-done.1.stash_ref
  58.1 0.0 collective-permute-done.5.grad_ref
  58.1 2.1 %backward.1 = (bf16[128,1024]{1,0:T(8,128)(2,1)}, bf16[128,128]{1,0:T(8,128)(2,1)}, bf16[128,128]{1,0:T(8,128)(2,1)}) custom-call(bf16[128,1280]{1,0:T(8,128)(2,1)S(1)} %collective-permute-done.1.stash_ref, bf16[128,1024]{1,0:T(8,128)(2,1)S(1)} %collective-permute-done.5.grad_ref, s32[1,128]{1,0:T(1,128)} %segments_ref.3), custom_call_target="tpu_custom_call" | custom-call | flops 7549747200 | bytes 1048576 | tf_op jit(solution)/shard_map/backward/pallas_call | solution.py:137
  60.2 0.0 collective-permute-done.4.fresh_ref
  60.2 0.0 collective-permute-done.3.late_ref
  60.2 1.8 %all-to-all-done.pieces_ref = bf16[8,16,1024]{2,1,0:T(8,128)(2,1)S(1)} async-done(((bf16[8,16,1024]{2,1,0:T(8,128)(2,1)}), bf16[8,16,1024]{2,1,0:T(8,128)(2,1)S(1)}, u32[]{:S(2)}, u32[]{:S(2)}) %all-to-all-start) | async-done | bytes 262176 | tf_op jit(solution)/shard_map/all_to_all | solution.py:168
  62.0 0.9 %finish.1 = (bf16[16,8192]{1,0:T(8,128)(2,1)}, bf16[128,1024]{1,0:T(8,128)(2,1)}, bf16[128,128]{1,0:T(8,128)(2,1)}, bf16[128,128]{1,0:T(8,128)(2,1)}) custom-call(bf16[8,16,1024]{2,1,0:T(8,128)(2,1)S(1)} %all-to-all-done.pieces_ref, bf16[128,1024]{1,0:T(8,128)(2,1)S(1)} %collective-permute-done.2.early_ref, ...), custom_call_target="tpu_custom_call" | custom-call | bytes 1048576 | tf_op jit(solution)/shard_map/finish/pallas_call | solution.py:97
Async XLA Ops:
  0.6 14.3 %copy-start = (bf16[1,128,1024]{2,1,0:T(8,128)(2,1)S(1)}, bf16[1,128,1024]{2,1,0:T(8,128)(2,1)}, u32[]{:S(2)}) copy-start(bf16[1,128,1024]{2,1,0:T(8,128)(2,1)} %param.9) | copy-start | bytes 786436
  0.6 16.2 %copy-start.1 = (bf16[1,128,1024]{2,1,0:T(8,128)(2,1)S(1)}, bf16[1,128,1024]{2,1,0:T(8,128)(2,1)}, u32[]{:S(2)}) copy-start(bf16[1,128,1024]{2,1,0:T(8,128)(2,1)} %param.17) | copy-start | bytes 786436
  2.7 19.9 %collective-permute-start = (bf16[128,1024]{1,0:T(8,128)(2,1)S(1)}, bf16[128,1024]{1,0:T(8,128)(2,1)}, u32[]{:S(2)}, u32[]{:S(2)}) collective-permute-start(bf16[128,1024]{1,0:T(8,128)(2,1)S(1)} %get-tuple-element.22), channel_id=1, source_target_pairs={{0,8},{1,9},{2,10},{3,11},{4,12},{5,13},{6,14},{7,15},{8,16},{9,17... | collective-permute-start | bytes 786440 | tf_op jit(solution)/shard_map/ppermute | solution.py:114
  6.1 52.0 %collective-permute-start.1 = (bf16[128,1280]{1,0:T(8,128)(2,1)S(1)}, bf16[128,1280]{1,0:T(8,128)(2,1)S(1)}, u32[]{:S(2)}, u32[]{:S(2)}) collective-permute-start(bf16[128,1280]{1,0:T(8,128)(2,1)S(1)} %get-tuple-element.23), channel_id=1, source_target_pairs={{0,504},{8,496},{16,488},{24,480},{32,472},{40,464},{48,456},{56,4... | collective-permute-start | bytes 983048 | tf_op jit(solution)/shard_map/ppermute | solution.py:155
  14.9 43.2 %collective-permute-start.2 = (bf16[128,1024]{1,0:T(8,128)(2,1)S(1)}, bf16[128,1024]{1,0:T(8,128)(2,1)S(1)}, u32[]{:S(2)}, u32[]{:S(2)}) collective-permute-start(bf16[128,1024]{1,0:T(8,128)(2,1)S(1)} %bitcast.17), channel_id=1, source_target_pairs={{0,504},{1,505},{8,496},{9,497},{16,488},{17,489},{24,480},{25,481... | collective-permute-start | bytes 786440 | tf_op jit(solution)/shard_map/ppermute | solution.py:157
  16.9 41.3 %collective-permute-start.5 = (bf16[128,1024]{1,0:T(8,128)(2,1)S(1)}, bf16[128,1024]{1,0:T(8,128)(2,1)S(1)}, u32[]{:S(2)}, u32[]{:S(2)}) collective-permute-start(bf16[128,1024]{1,0:T(8,128)(2,1)S(1)} %bitcast.23), channel_id=1, source_target_pairs={{0,504},{8,0},{16,8},{24,16},{32,24},{40,32},{48,40},{56,48},{64,5... | collective-permute-start | bytes 786440 | tf_op jit(solution)/shard_map/ppermute | solution.py:149
  22.6 39.5 %all-to-all-start = ((bf16[8,16,1024]{2,1,0:T(8,128)(2,1)}), bf16[8,16,1024]{2,1,0:T(8,128)(2,1)S(1)}, u32[]{:S(2)}, u32[]{:S(2)}) async-start(bf16[8,16,1024]{2,1,0:T(8,128)(2,1)} %bitcast.6), calls=%async_computation | async-start | bytes 524288 | tf_op jit(solution)/shard_map/all_to_all | solution.py:168
  32.4 27.8 %collective-permute-start.3 = (bf16[128,1024]{1,0:T(8,128)(2,1)S(1)}, bf16[128,1024]{1,0:T(8,128)(2,1)S(1)}, u32[]{:S(2)}, u32[]{:S(2)}) collective-permute-start(bf16[128,1024]{1,0:T(8,128)(2,1)S(1)} %bitcast.18), channel_id=1, source_target_pairs={{2,506},{3,507},{4,508},{5,509},{6,510},{7,511},{10,498},{11,499},... | collective-permute-start | bytes 786440 | tf_op jit(solution)/shard_map/ppermute | solution.py:157
  33.0 27.2 %collective-permute-start.4 = (bf16[128,256]{1,0:T(8,128)(2,1)S(1)}, bf16[128,256]{1,0:T(8,128)(2,1)S(1)}, u32[]{:S(2)}, u32[]{:S(2)}) collective-permute-start(bf16[128,256]{1,0:T(8,128)(2,1)S(1)} %get-tuple-element.25), channel_id=1, source_target_pairs={{0,504},{8,496},{16,488},{24,480},{32,472},{40,464},{48,456},{56,4... | collective-permute-start | bytes 196616 | tf_op jit(solution)/shard_map/ppermute | solution.py:155

commit v7 on v5

--- a/solution.py
+++ b/solution.py
@@ -43,16 +43,17 @@
     prob = probability(stacked(q_ref, width), k_ref[...], segments_ref[...])
     stash_ref[:, :width] = held_q_ref[...]
     stash_ref[:, width : width + HD] = held_k_ref[...]
-    stash_ref[:, width + HD :] = held_v_ref[...]
-    fresh_ref[:, :HD] = k_ref[...]
-    fresh_ref[:, HD:] = v_ref[...]
+    stash_ref[:, width + HD : width + 2 * HD] = held_v_ref[...]
+    stash_ref[:, width + 2 * HD :] = k_ref[...]
+    fresh_ref[...] = v_ref[...]
     unstack(out_ref, contract(prob.astype(jnp.bfloat16), v_ref[...], 0, 0).astype(jnp.bfloat16))
 
 
-def backward_kernel(stash_ref, grad_ref, segments_ref, grad_q_ref, grad_k_ref, grad_v_ref):
+def backward_kernel(stash_ref, grad_ref, segments_ref, grad_q_ref, grad_k_ref, grad_v_ref, fresh_k_ref):
     width = grad_ref.shape[1]
+    fresh_k_ref[...] = stash_ref[:, width + 2 * HD :]
     queries, grads = stacked(stash_ref, width), stacked(grad_ref, width)
-    keys, values = stash_ref[:, width : width + HD], stash_ref[:, width + HD :]
+    keys, values = stash_ref[:, width : width + HD], stash_ref[:, width + HD : width + 2 * HD]
     prob = probability(queries, keys, segments_ref[...])
     dprob = contract(values, grads, 1, 1)
     delta = jnp.sum(prob * dprob, axis=0, keepdims=True)
@@ -66,14 +67,13 @@
     return jax.ShapeDtypeStruct((rows, columns), jnp.bfloat16)
 
 
-def finish_kernel(pieces_ref, early_ref, late_ref, fresh_ref, passed_ref, q_ref, k_ref, v_ref):
+def finish_kernel(pieces_ref, early_ref, late_ref, fresh_ref, passed_ref, q_ref, v_ref):
     parts, _, width = pieces_ref.shape
     late = jnp.where(lax.rem(lax.axis_index("section"), 16) == 0, parts - 2, 0)
     for part in range(parts):
         column = pl.multiple_of(lax.rem(part + late, parts) * width, width)
         passed_ref[:, pl.ds(column, width)] = pieces_ref[part]
-    k_ref[...] = fresh_ref[:, :HD]
-    v_ref[...] = fresh_ref[:, HD:]
+    v_ref[...] = fresh_ref[...]
     is_early = lax.axis_index("tp") < 2
 
     @pl.when(is_early)
@@ -91,9 +91,9 @@
     arrays = (pltpu.with_memory_space_constraint(x, pltpu.VMEM) for x in (pieces, early, late, fresh))
     return pl.pallas_call(
         finish_kernel,
-        out_shape=(like(rows, parts * width), like(tokens, width), like(tokens, HD), like(tokens, HD)),
+        out_shape=(like(rows, parts * width), like(tokens, width), like(tokens, HD)),
         in_specs=[VMEM] * 4,
-        out_specs=(VMEM,) * 4,
+        out_specs=(VMEM,) * 3,
         cost_estimate=pl.CostEstimate(flops=0, bytes_accessed=8 * parts * rows * width, transcendentals=0),
         name="finish",
     )(*arrays)
@@ -118,7 +118,7 @@
     whole = width + 2 * HD
     return pl.pallas_call(
         forward_kernel,
-        out_shape=(held_in_vmem(rows, width), held_in_vmem(rows, whole), held_in_vmem(rows, 2 * HD)),
+        out_shape=(held_in_vmem(rows, width), held_in_vmem(rows, whole + HD), held_in_vmem(rows, HD)),
         in_specs=[VMEM] * 7,
         out_specs=(VMEM,) * 3,
         cost_estimate=pl.CostEstimate(flops=FORWARD_FLOPS * rows * rows * width, bytes_accessed=20 * rows * width, transcendentals=rows * width),
@@ -130,9 +130,9 @@
     rows, width = grad.shape
     return pl.pallas_call(
         backward_kernel,
-        out_shape=(like(rows, width),) + (like(rows, HD),) * 2,
+        out_shape=(like(rows, width),) + (like(rows, HD),) * 3,
         in_specs=[VMEM] * 3,
-        out_specs=(VMEM,) * 3,
+        out_specs=(VMEM,) * 4,
         cost_estimate=pl.CostEstimate(flops=BACKWARD_FLOPS * rows * rows * width, bytes_accessed=8 * rows * width, transcendentals=rows * width),
         name="backward",
     )(pltpu.with_memory_space_constraint(stash, pltpu.VMEM), pltpu.with_memory_space_constraint(grad, pltpu.VMEM), segments)
@@ -162,9 +162,9 @@
     pieces = lax.all_to_all(out, "tp", split_axis=0, concat_axis=0)
     late_q = mirrored(fwd_q[0], lines[1:])
     stash, early_q = lax.optimization_barrier((stash, early_q))
-    grad_q, grad_k, grad_v = backward(stash, arriving, back_segments)
+    grad_q, grad_k, grad_v, evicted_k = backward(stash, arriving, back_segments)
     late_q, fresh, grad_k = lax.optimization_barrier((late_q, mirrored(fresh), grad_k))
-    passed, evicted_q, evicted_k, evicted_v = finish(pieces, early_q, late_q, fresh)
+    passed, evicted_q, evicted_v = finish(pieces, early_q, late_q, fresh)
     return tuple(x[None] for x in (passed, evicted_q, evicted_k, evicted_v, grad_q, grad_k, grad_v))
 
 

time: 63 us -> 63.7 us (1.011)
  starting transfers between devices: 34.5 us -> 35.2 us
    ppermute x2, starting transfers between devices: 13.1 us -> 13.8 us  [mirrored(): lax.ppermute(value, 'section', [(i, count - 1 - i) for i in range(count)])]
where the time goes in v7:
time: 63.7 us; the launch traced here: 63.3 us
  starting transfers between devices  35.2 us (55%)
  waiting for transfers between devices  22.7 us (36%)
  Pallas kernels  4.67 us (7%)
  between operations  0.74 us (1%)
    ppermute x2, waiting for transfers between devices, mirrored(): return lax.ppermute(value, ('section', 'tp'), pairs)  20.5 us
    ppermute x2, starting transfers between devices, mirrored(): lax.ppermute(value, 'section', [(i, count - 1 - i) for i in range(count)])  13.8 us
    all_to_all x1, starting transfers between devices, shards(): pieces = lax.all_to_all(out, 'tp', split_axis=0, concat_axis=0)  9.78 us
    ppermute x1, starting transfers between devices, shifted(): lax.ppermute(value, 'section', [(i, (i + steps) % count) for i in range(c...  5.68 us
    ppermute x1, starting transfers between devices, handed_on(): return lax.ppermute(value, ('section', 'tp'), pairs)  3.4 us
    ppermute x2, starting transfers between devices, mirrored(): return lax.ppermute(value, ('section', 'tp'), pairs)  2.59 us
    all_to_all x1, waiting for transfers between devices, shards(): pieces = lax.all_to_all(out, 'tp', split_axis=0, concat_axis=0)  2.2 us
    pallas_call x1, Pallas kernels, backward(): pl.pallas_call(backward_kernel, out_shape=(like(rows, width),) + (like(ro...  2.07 us
  transfers between devices with their start and end apart: 7, of which 2 were waited for; matrix products, arithmetic and copies ran while one was open for 0% of the time, Pallas kernels for 3%

profile of v7, /device:TPU:32, one launch (start us, length us, event | category | flops | bytes accessed | tf_op | source)
XLA Modules:
  0.0 63.3 jit_solution(15584008118645518720)
XLA Ops:
  0.6 0.0 copy-start
  0.6 0.0 copy-start.1
  0.7 1.8 %forward.1 = (bf16[128,1024]{1,0:T(8,128)(2,1)S(1)}, bf16[128,1408]{1,0:T(8,128)(2,1)S(1)}, bf16[128,128]{1,0:T(8,128)(2,1)S(1)}) custom-call(bf16[128,1024]{1,0:T(8,128)(2,1)} %bitcast.16, bf16[128,128]{1,0:T(8,128)(2,1)} %bitcast.19, bf16[128,128]{1,0:T(8,128)(2,1)} %bitcast.20, s32[1,128]{1,0:T(1,128)} %segments_ref.2, bf16[128,1024]{1,0:T(8,128)(2,1)} %bitcast.15, ...), custom_call_target="tpu_custom_call" | custom-call | flops 67108864 | bytes 2621440 | tf_op jit(solution)/shard_map/forward/pallas_call | solution.py:119
  2.4 3.4 %collective-permute-start = (bf16[128,1024]{1,0:T(8,128)(2,1)S(1)}, bf16[128,1024]{1,0:T(8,128)(2,1)}, u32[]{:S(2)}, u32[]{:S(2)}) collective-permute-start(bf16[128,1024]{1,0:T(8,128)(2,1)S(1)} %get-tuple-element.22), channel_id=1, source_target_pairs={{0,8},{1,9},{2,10},{3,11},{4,12},{5,13},{6,14},{7,15},{8,16},{9,17... | collective-permute-start | bytes 786440 | tf_op jit(solution)/shard_map/ppermute | solution.py:109
  5.8 8.8 %collective-permute-start.1 = (bf16[128,1408]{1,0:T(8,128)(2,1)S(1)}, bf16[128,1408]{1,0:T(8,128)(2,1)S(1)}, u32[]{:S(2)}, u32[]{:S(2)}) collective-permute-start(bf16[128,1408]{1,0:T(8,128)(2,1)S(1)} %get-tuple-element.23), channel_id=1, source_target_pairs={{0,504},{8,496},{16,488},{24,480},{32,472},{40,464},{48,456},{56,4... | collective-permute-start | bytes 1081352 | tf_op jit(solution)/shard_map/ppermute | solution.py:149
  14.6 0.0 copy-done
  14.7 1.9 %collective-permute-start.2 = (bf16[128,1024]{1,0:T(8,128)(2,1)S(1)}, bf16[128,1024]{1,0:T(8,128)(2,1)S(1)}, u32[]{:S(2)}, u32[]{:S(2)}) collective-permute-start(bf16[128,1024]{1,0:T(8,128)(2,1)S(1)} %bitcast.17), channel_id=1, source_target_pairs={{0,504},{1,505},{8,496},{9,497},{16,488},{17,489},{24,480},{25,481... | collective-permute-start | bytes 786440 | tf_op jit(solution)/shard_map/ppermute | solution.py:151
  16.6 0.0 copy-done.1
  16.6 5.7 %collective-permute-start.5 = (bf16[128,1024]{1,0:T(8,128)(2,1)S(1)}, bf16[128,1024]{1,0:T(8,128)(2,1)S(1)}, u32[]{:S(2)}, u32[]{:S(2)}) collective-permute-start(bf16[128,1024]{1,0:T(8,128)(2,1)S(1)} %bitcast.23), channel_id=1, source_target_pairs={{0,504},{8,0},{16,8},{24,16},{32,24},{40,32},{48,40},{56,48},{64,5... | collective-permute-start | bytes 786440 | tf_op jit(solution)/shard_map/ppermute | solution.py:143
  22.3 0.0 collective-permute-done
  22.3 9.8 %all-to-all-start = ((bf16[8,16,1024]{2,1,0:T(8,128)(2,1)}), bf16[8,16,1024]{2,1,0:T(8,128)(2,1)S(1)}, u32[]{:S(2)}, u32[]{:S(2)}) async-start(bf16[8,16,1024]{2,1,0:T(8,128)(2,1)} %bitcast.6), calls=%async_computation | async-start | bytes 524288 | tf_op jit(solution)/shard_map/all_to_all | solution.py:162
  32.1 0.7 %collective-permute-start.3 = (bf16[128,1024]{1,0:T(8,128)(2,1)S(1)}, bf16[128,1024]{1,0:T(8,128)(2,1)S(1)}, u32[]{:S(2)}, u32[]{:S(2)}) collective-permute-start(bf16[128,1024]{1,0:T(8,128)(2,1)S(1)} %bitcast.18), channel_id=1, source_target_pairs={{2,506},{3,507},{4,508},{5,509},{6,510},{7,511},{10,498},{11,499},... | collective-permute-start | bytes 786440 | tf_op jit(solution)/shard_map/ppermute | solution.py:151
  32.7 4.9 %collective-permute-start.4 = (bf16[128,128]{1,0:T(8,128)(2,1)S(1)}, bf16[128,128]{1,0:T(8,128)(2,1)S(1)}, u32[]{:S(2)}, u32[]{:S(2)}) collective-permute-start(bf16[128,128]{1,0:T(8,128)(2,1)S(1)} %get-tuple-element.25), channel_id=1, source_target_pairs={{0,504},{8,496},{16,488},{24,480},{32,472},{40,464},{48,456},{56,4... | collective-permute-start | bytes 98312 | tf_op jit(solution)/shard_map/ppermute | solution.py:149
  37.7 20.5 %collective-permute-done.2.early_ref = bf16[128,1024]{1,0:T(8,128)(2,1)S(1)} collective-permute-done((bf16[128,1024]{1,0:T(8,128)(2,1)S(1)}, bf16[128,1024]{1,0:T(8,128)(2,1)S(1)}, u32[]{:S(2)}, u32[]{:S(2)}) %collective-permute-start.2) | collective-permute-done | bytes 262176 | tf_op jit(solution)/shard_map/ppermute | solution.py:151
  58.2 0.0 collective-permute-done.1.stash_ref
  58.2 0.0 collective-permute-done.5.grad_ref
  58.2 2.1 %backward.1 = (bf16[128,1024]{1,0:T(8,128)(2,1)}, bf16[128,128]{1,0:T(8,128)(2,1)}, bf16[128,128]{1,0:T(8,128)(2,1)}, bf16[128,128]{1,0:T(8,128)(2,1)}) custom-call(bf16[128,1408]{1,0:T(8,128)(2,1)S(1)} %collective-permute-done.1.stash_ref, bf16[128,1024]{1,0:T(8,128)(2,1)S(1)} %collective-permute-done.5.grad_ref, s32[1,128]{1,0:T(1,128)} %segments_ref.3), custom_call_target="tpu_custom_call" | custom-call | flops 7549747200 | bytes 1048576 | tf_op jit(solution)/shard_map/backward/pallas_call | solution.py:131
  60.2 0.0 collective-permute-done.4.fresh_ref
  60.3 0.0 collective-permute-done.3.late_ref
  60.3 2.2 %all-to-all-done.pieces_ref = bf16[8,16,1024]{2,1,0:T(8,128)(2,1)S(1)} async-done(((bf16[8,16,1024]{2,1,0:T(8,128)(2,1)}), bf16[8,16,1024]{2,1,0:T(8,128)(2,1)S(1)}, u32[]{:S(2)}, u32[]{:S(2)}) %all-to-all-start) | async-done | bytes 262176 | tf_op jit(solution)/shard_map/all_to_all | solution.py:162
  62.5 0.8 %finish.1 = (bf16[16,8192]{1,0:T(8,128)(2,1)}, bf16[128,1024]{1,0:T(8,128)(2,1)}, bf16[128,128]{1,0:T(8,128)(2,1)}) custom-call(bf16[8,16,1024]{2,1,0:T(8,128)(2,1)S(1)} %all-to-all-done.pieces_ref, bf16[128,1024]{1,0:T(8,128)(2,1)S(1)} %collective-permute-done.2.early_ref, bf16[128,1024]{1,0:T(8,128)(2,1)S(1)} %collective-permute-done.3.late_ref, ...), custom_call_target="tpu_custom_call" | custom-call | bytes 1048576 | tf_op jit(solution)/shard_map/finish/pallas_call | solution.py:92
Async XLA Ops:
  0.6 14.0 %copy-start = (bf16[1,128,1024]{2,1,0:T(8,128)(2,1)S(1)}, bf16[1,128,1024]{2,1,0:T(8,128)(2,1)}, u32[]{:S(2)}) copy-start(bf16[1,128,1024]{2,1,0:T(8,128)(2,1)} %param.9) | copy-start | bytes 786436
  0.6 15.9 %copy-start.1 = (bf16[1,128,1024]{2,1,0:T(8,128)(2,1)S(1)}, bf16[1,128,1024]{2,1,0:T(8,128)(2,1)}, u32[]{:S(2)}) copy-start(bf16[1,128,1024]{2,1,0:T(8,128)(2,1)} %param.17) | copy-start | bytes 786436
  2.4 19.9 %collective-permute-start = (bf16[128,1024]{1,0:T(8,128)(2,1)S(1)}, bf16[128,1024]{1,0:T(8,128)(2,1)}, u32[]{:S(2)}, u32[]{:S(2)}) collective-permute-start(bf16[128,1024]{1,0:T(8,128)(2,1)S(1)} %get-tuple-element.22), channel_id=1, source_target_pairs={{0,8},{1,9},{2,10},{3,11},{4,12},{5,13},{6,14},{7,15},{8,16},{9,17... | collective-permute-start | bytes 786440 | tf_op jit(solution)/shard_map/ppermute | solution.py:109
  5.8 52.4 %collective-permute-start.1 = (bf16[128,1408]{1,0:T(8,128)(2,1)S(1)}, bf16[128,1408]{1,0:T(8,128)(2,1)S(1)}, u32[]{:S(2)}, u32[]{:S(2)}) collective-permute-start(bf16[128,1408]{1,0:T(8,128)(2,1)S(1)} %get-tuple-element.23), channel_id=1, source_target_pairs={{0,504},{8,496},{16,488},{24,480},{32,472},{40,464},{48,456},{56,4... | collective-permute-start | bytes 1081352 | tf_op jit(solution)/shard_map/ppermute | solution.py:149
  14.7 43.5 %collective-permute-start.2 = (bf16[128,1024]{1,0:T(8,128)(2,1)S(1)}, bf16[128,1024]{1,0:T(8,128)(2,1)S(1)}, u32[]{:S(2)}, u32[]{:S(2)}) collective-permute-start(bf16[128,1024]{1,0:T(8,128)(2,1)S(1)} %bitcast.17), channel_id=1, source_target_pairs={{0,504},{1,505},{8,496},{9,497},{16,488},{17,489},{24,480},{25,481... | collective-permute-start | bytes 786440 | tf_op jit(solution)/shard_map/ppermute | solution.py:151
  16.6 41.6 %collective-permute-start.5 = (bf16[128,1024]{1,0:T(8,128)(2,1)S(1)}, bf16[128,1024]{1,0:T(8,128)(2,1)S(1)}, u32[]{:S(2)}, u32[]{:S(2)}) collective-permute-start(bf16[128,1024]{1,0:T(8,128)(2,1)S(1)} %bitcast.23), channel_id=1, source_target_pairs={{0,504},{8,0},{16,8},{24,16},{32,24},{40,32},{48,40},{56,48},{64,5... | collective-permute-start | bytes 786440 | tf_op jit(solution)/shard_map/ppermute | solution.py:143
  22.3 40.2 %all-to-all-start = ((bf16[8,16,1024]{2,1,0:T(8,128)(2,1)}), bf16[8,16,1024]{2,1,0:T(8,128)(2,1)S(1)}, u32[]{:S(2)}, u32[]{:S(2)}) async-start(bf16[8,16,1024]{2,1,0:T(8,128)(2,1)} %bitcast.6), calls=%async_computation | async-start | bytes 524288 | tf_op jit(solution)/shard_map/all_to_all | solution.py:162
  32.1 28.2 %collective-permute-start.3 = (bf16[128,1024]{1,0:T(8,128)(2,1)S(1)}, bf16[128,1024]{1,0:T(8,128)(2,1)S(1)}, u32[]{:S(2)}, u32[]{:S(2)}) collective-permute-start(bf16[128,1024]{1,0:T(8,128)(2,1)S(1)} %bitcast.18), channel_id=1, source_target_pairs={{2,506},{3,507},{4,508},{5,509},{6,510},{7,511},{10,498},{11,499},... | collective-permute-start | bytes 786440 | tf_op jit(solution)/shard_map/ppermute | solution.py:151
  32.7 27.5 %collective-permute-start.4 = (bf16[128,128]{1,0:T(8,128)(2,1)S(1)}, bf16[128,128]{1,0:T(8,128)(2,1)S(1)}, u32[]{:S(2)}, u32[]{:S(2)}) collective-permute-start(bf16[128,128]{1,0:T(8,128)(2,1)S(1)} %get-tuple-element.25), channel_id=1, source_target_pairs={{0,504},{8,496},{16,488},{24,480},{32,472},{40,464},{48,456},{56,4... | collective-permute-start | bytes 98312 | tf_op jit(solution)/shard_map/ppermute | solution.py:149
